TPU v7x, 32 devices: a whole 2x2x4 slice. The times are simulated.
32 devices in a mesh: bx: 8 (over z, y), by: 4 (over x, core).
Axes of the slice: x: 2, y: 2, z: 4, core: 2. Of those that a mesh axis runs over, the one named last changes fastest.
Arguments:
- source: float32 [8, 4, 6, 8192], P('bx', 'by'), may hold values from -6 to 6
- lists: int32 [8, 4, 4], P(None, 'by'), may hold values from 0 to 7, as said below
- voxel_slot: int32 [8, 4, 16384], P('bx', 'by'), may hold values from 0 to 3
- voxel_cell: int32 [8, 4, 16384], P('bx', 'by'), may hold values from 0 to 7038, as said below
- frac: float32 [8, 4, 3, 16384], P('bx', 'by'), may hold values from 0 to 1
- displace: float32 [3, 64, 16, 512], P(None, None, 'bx', 'by'), may hold values from -0.25 to 0.25
Outputs:
- warped: float32 [8, 4, 6, 16384], P('bx', 'by')
Inputs may be any that keep to these rules, and one draw needn't show every extreme that they name: `lists`: each target block's 4 entries are distinct slab groups. `voxel_cell`: each is ix * 8 * 128 + iy * 128 + iz with ix < 7, iy < 7, iz < 127.
All inputs are finite; a program needn't handle non-finite values.
Results may differ from a plain program's by a relative error of at most 0.00007.
Values sent between devices are 32-bit elements; how exact they have to be, the bound alone decides.
No kernel may reach another device: no remote copies, remote signals or barrier semaphores. Data moves between devices by JAX's collectives and lax.ppermute only.
A program may use at most 64 MiB of HBM per device.

v0:
```python
import jax
import jax.numpy as jnp
from jax import lax
from jax.experimental import pallas as pl
from jax.experimental.pallas import tpu as pltpu
from jax.sharding import PartitionSpec as P

PX = 8
PY = 8
PZ = 128
STEPS = 2


def with_halo(cells, sides, width):
    for axis, dim in sides:
        count = lax.axis_size(axis)
        ends = count - 1
        head = lax.slice_in_dim(cells, 0, width, axis=dim)
        tail = lax.slice_in_dim(cells, cells.shape[dim] - width, cells.shape[dim], axis=dim)
        cells = jnp.concatenate(
            [
                lax.ppermute(tail, axis, [(i, (i + 1) % count) for i in range(ends)]),
                cells,
                lax.ppermute(head, axis, [((i + 1) % count, i) for i in range(ends)]),
            ],
            axis=dim,
        )
    return cells


def gradients(padded):
    full = jnp.pad(padded, ((0, 0), (1, 1), (0, 0), (0, 0)))
    grad_x = 0.5 * (full[:, 1:-1, 2:, 1:-1] - full[:, 1:-1, :-2, 1:-1])
    grad_y = 0.5 * (full[:, 1:-1, 1:-1, 2:] - full[:, 1:-1, 1:-1, :-2])
    grad_z = 0.5 * (full[:, 2:, 1:-1, 1:-1] - full[:, :-2, 1:-1, 1:-1])
    return [grad_x, grad_y, grad_z]


def jacobian_matrix(gradient_list):
    return [
        [
            gradient_list[second_axis][first_axis] + (1.0 if first_axis == second_axis else 0.0)
            for second_axis in range(3)
        ]
        for first_axis in range(3)
    ]


def transpose_inverse(matrix):
    cof_00 = matrix[1][1] * matrix[2][2] - matrix[1][2] * matrix[2][1]
    cof_01 = -(matrix[1][0] * matrix[2][2] - matrix[1][2] * matrix[2][0])
    cof_02 = matrix[1][0] * matrix[2][1] - matrix[1][1] * matrix[2][0]
    cof_10 = -(matrix[0][1] * matrix[2][2] - matrix[0][2] * matrix[2][1])
    cof_11 = matrix[0][0] * matrix[2][2] - matrix[0][2] * matrix[2][0]
    cof_12 = -(matrix[0][0] * matrix[2][1] - matrix[0][1] * matrix[2][0])
    cof_20 = matrix[0][1] * matrix[1][2] - matrix[0][2] * matrix[1][1]
    cof_21 = -(matrix[0][0] * matrix[1][2] - matrix[0][2] * matrix[1][0])
    cof_22 = matrix[0][0] * matrix[1][1] - matrix[0][1] * matrix[1][0]
    determinant = matrix[0][0] * cof_00 + matrix[0][1] * cof_01 + matrix[0][2] * cof_02
    reciprocal = 1.0 / determinant
    return [
        [cof_00 * reciprocal, cof_01 * reciprocal, cof_02 * reciprocal],
        [cof_10 * reciprocal, cof_11 * reciprocal, cof_12 * reciprocal],
        [cof_20 * reciprocal, cof_21 * reciprocal, cof_22 * reciprocal],
    ]


def polar_factor(jacobian):
    rotation = jacobian
    for repeat in range(STEPS):
        inverse = transpose_inverse(rotation)
        rotation = [
            [
                0.5 * (rotation[first_axis][second_axis] + inverse[first_axis][second_axis])
                for second_axis in range(3)
            ]
            for first_axis in range(3)
        ]
    return rotation


def reorient(rotation, components):
    tensor = [
        [components[0], components[3], components[4]],
        [components[3], components[1], components[5]],
        [components[4], components[5], components[2]],
    ]
    left = [
        [
            rotation[first_axis][0] * tensor[0][second_axis]
            + rotation[first_axis][1] * tensor[1][second_axis]
            + rotation[first_axis][2] * tensor[2][second_axis]
            for second_axis in range(3)
        ]
        for first_axis in range(3)
    ]

    def entry(first_axis, second_axis):
        return (
            left[first_axis][0] * rotation[second_axis][0]
            + left[first_axis][1] * rotation[second_axis][1]
            + left[first_axis][2] * rotation[second_axis][2]
        )

    return [entry(0, 0), entry(1, 1), entry(2, 2), entry(0, 1), entry(0, 2), entry(1, 2)]


def sample_kernel(slab_ref, table_ref, slot_ref, cell_ref, frac_ref, out_ref):
    slots = slab_ref.shape[0]
    groups = slot_ref.shape[0]
    row_iota = lax.broadcasted_iota(jnp.int32, (PY, PZ), 0)

    def spread(row):
        return jnp.broadcast_to(row, (PY, PZ))

    def group(g, carry):
        slot = spread(slot_ref[pl.ds(g, 1), :])
        cell = spread(cell_ref[pl.ds(g, 1), :])
        along_x = spread(frac_ref[0, pl.ds(g, 1), :])
        along_y = spread(frac_ref[1, pl.ds(g, 1), :])
        along_z = spread(frac_ref[2, pl.ds(g, 1), :])
        iz = cell & (PZ - 1)
        iy = (cell // PZ) & (PY - 1)
        ix = cell // (PY * PZ)
        weight_y = jnp.where(row_iota == iy, 1.0 - along_y, jnp.where(row_iota == iy + 1, along_y, 0.0))
        code = slot * PX + ix

        def one_slot(s, totals):
            slab = slab_ref[s]
            totals = list(totals)
            for x in range(PX):
                here = s * PX + x
                weight = jnp.where(code == here, 1.0 - along_x, 0.0)
                if x > 0:
                    weight = jnp.where(code == here - 1, along_x, weight)
                for c in range(6):
                    part = table_ref[slab, c * PX + x]
                    lower = jnp.take_along_axis(part, iz, axis=1, mode="promise_in_bounds")
                    upper = jnp.take_along_axis(part, iz + 1, axis=1, mode="promise_in_bounds")
                    totals[c] = totals[c] + weight * lower
                    totals[6 + c] = totals[6 + c] + weight * upper
            return tuple(totals)

        zero = jnp.zeros((PY, PZ), jnp.float32)
        totals = lax.fori_loop(0, slots, one_slot, (zero,) * 12)
        rows = [
            jnp.sum((totals[c] * (1.0 - along_z) + totals[6 + c] * along_z) * weight_y, axis=0, keepdims=True)
            for c in range(6)
        ]
        out_ref[pl.ds(g, 1)] = jnp.concatenate(rows, axis=0)[None]
        return carry

    lax.fori_loop(0, groups, group, 0)


def on_device(source, lists, voxel_slot, voxel_cell, frac, displace):
    count = lax.axis_size("bx")
    row_index = lax.axis_index("bx")
    voxels = voxel_cell.shape[2]
    groups = voxels // PZ
    table = source.reshape(6 * PX * PY, PZ)
    my_slabs = lax.dynamic_index_in_dim(lists[:, 0, :], row_index, 0, keepdims=False)
    line = lax.all_gather(
        table, "bx", axis=0, axis_index_groups=[list(range(k, count, 2)) for k in range(2)]
    )
    across = lax.ppermute(line, "bx", [(i, i ^ 1) for i in range(count)])
    odd = row_index % 2 == 1
    blocks = jnp.stack([jnp.where(odd, across, line), jnp.where(odd, line, across)], axis=1)
    blocks = blocks.reshape(count, 6 * PX, PY, PZ)
    vmem = pl.BlockSpec(memory_space=pltpu.VMEM)
    sample = pl.pallas_call(
        sample_kernel,
        out_shape=jax.ShapeDtypeStruct((groups, 6, PZ), jnp.float32),
        in_specs=[pl.BlockSpec(memory_space=pltpu.SMEM)] + [vmem] * 4,
        out_specs=vmem,
        compiler_params=pltpu.CompilerParams(vmem_limit_bytes=32 * 2**20),
    )(
        my_slabs,
        blocks,
        voxel_slot.reshape(groups, PZ),
        voxel_cell.reshape(groups, PZ),
        frac.reshape(3, groups, PZ),
    )
    padded = with_halo(displace, (("bx", 2), ("by", 3)), 1)
    gradient_list = [field.reshape(3, groups, PZ) for field in gradients(padded)]
    rotation = polar_factor(jacobian_matrix(gradient_list))
    result = reorient(rotation, [sample[:, index] for index in range(6)])
    return jnp.stack(result, 0).reshape(1, 1, 6, voxels)


def solution(mesh):
    return jax.shard_map(
        on_device,
        mesh=mesh,
        in_specs=(
            P("bx", "by", None, None),
            P(None, "by", None),
            P("bx", "by", None),
            P("bx", "by", None),
            P("bx", "by", None, None),
            P(None, None, "bx", "by"),
        ),
        out_specs=P("bx", "by", None, None),
        check_vma=False,
    )
```

profile of v0, /device:TPU:0, one launch (start us, length us, event | category | flops | bytes accessed | tf_op | source)
XLA Modules:
  0.0 157.6 jit_solution(10212608254644224338)
XLA Ops:
  0.0 0.0 copy-start
  0.0 0.0 copy-start.5
  0.0 1.2 fusion.10
  1.2 1.3 collective-permute-start
  2.5 0.0 copy-start.4
  2.6 5.6 %collective-permute-start.1 = (f32[3,64,1,128]{3,2,1,0:T(1,128)S(1)}, f32[3,64,1,128]{3,2,1,0:T(1,128)S(1)}, u32[]{:S(2)}, u32[]{:S(2)}) collective-permute-start(f32[3,64,1,128]{3,2,1,0:T(1,128)S(1)} %get-tuple-element.50), channel_id=1, source_target_pairs={{0,4},{4,8},{8,12},{12,16},{16,20},{20,24},{24,28},{1,5},{5,9},{9,... | collective-permute-start | bytes 294920 | tf_op jit(solution)/shard_map/ppermute | solution.py:22
  8.2 0.7 collective-permute-done
  8.9 2.3 %collective-permute-done.1 = f32[3,64,1,128]{3,2,1,0:T(1,128)S(1)} collective-permute-done((f32[3,64,1,128]{3,2,1,0:T(1,128)S(1)}, f32[3,64,1,128]{3,2,1,0:T(1,128)S(1)}, u32[]{:S(2)}, u32[]{:S(2)}) %collective-permute-start.1) | collective-permute-done | bytes 98336 | tf_op jit(solution)/shard_map/ppermute | solution.py:22
  11.2 1.2 pad_maximum_fusion.1
  12.4 0.3 fusion.6
  12.7 1.3 collective-permute-start.2
  14.0 3.1 %collective-permute-start.3 = (f32[3,64,4,1]{3,2,1,0:T(4,128)S(1)}, f32[3,64,4,1]{3,2,1,0:T(4,128)S(1)}, u32[]{:S(2)}, u32[]{:S(2)}) collective-permute-start(f32[3,64,4,1]{3,2,1,0:T(4,128)S(1)} %get-tuple-element.39), channel_id=1, source_target_pairs={{0,1},{1,2},{2,3},{4,5},{5,6},{6,7},{8,9},{9,10},{10,11},{12,13},{... | collective-permute-start | bytes 9224 | tf_op jit(solution)/shard_map/ppermute | solution.py:22
  17.1 0.0 copy-done.5
  17.1 22.2 %all_gather.3 = f32[4,384,128]{2,1,0:T(8,128)S(1)} all-gather(f32[1,384,128]{2,1,0:T(8,128)S(1)} %bitcast.157), channel_id=1, replica_groups={{0,8,16,24},{4,12,20,28},{1,9,17,25},{5,13,21,29},{2,10,18,26},{6,14,22..., dimensions={0}, use_global_device_ids=true | all-gather | bytes 983040 | tf_op jit(solution)/shard_map/all_gather | solution.py:163
  39.3 0.0 collective-permute-start.4
  39.3 0.0 copy-done
  39.3 0.2 dynamic-slice_reduce_fusion.slab_ref
  39.4 0.0 collective-permute-done.2
  39.4 0.0 collective-permute-done.3
  39.5 0.0 copy-done.4
  39.5 1.5 select_maximum_fusion
  41.0 0.5 fusion.1
  41.5 1.8 %fusion.5 = (f32[3,64,2,128]{3,2,1,0:T(2,128)S(1)}, f32[3,64,2,128]{3,2,1,0:T(2,128)S(1)}) fusion(f32[3,64,2,128]{3,2,1,0:T(2,128)S(1)} %copy-done.4, f32[3,64,1,128]{3,2,1,0:T(1,128)S(1)} %collective-permute-done.1, f32[3,64,1,128]{3,2,1,0:T(1,128)S(1)} %collective-permute-done, f32[3,64,4,1]{3,2,1,0:T(4,128)S(1)} %collective-permute-done.3, ...), kind=kLoop, calls=%fused_computation.23 | loop fusion | flops 589824 | bytes 792576 | tf_op jit(solution)/shard_map/mul | solution.py:33
  43.3 0.1 fusion.8
  43.4 0.8 multiply_subtract_fusion.1
  44.2 0.7 add_multiply_fusion.8
  44.9 0.2 add_multiply_fusion.7
  45.1 12.9 %collective-permute-done.4 = f32[4,384,128]{2,1,0:T(8,128)S(1)} collective-permute-done((f32[4,384,128]{2,1,0:T(8,128)S(1)}, f32[4,384,128]{2,1,0:T(8,128)S(1)}, u32[]{:S(2)}, u32[]{:S(2)}) %collective-permute-start.4) | collective-permute-done | bytes 786464 | tf_op jit(solution)/shard_map/ppermute | solution.py:166
  58.0 0.1 select_bitcast_fusion.1
  58.1 0.1 pad_maximum_fusion
  58.2 0.0 copy-start.1
  58.2 0.0 copy-start.2
  58.2 0.0 copy-start.3
  58.3 0.1 copy.35
  58.4 0.8 copy-done.1
  59.1 0.0 copy-done.2
  59.2 0.0 copy-done.3
  59.2 94.0 %shard_map.64 = f32[128,6,128]{2,1,0:T(8,128)S(1)} custom-call(s32[4]{0:T(128)S(1)} %dynamic-slice_reduce_fusion.slab_ref, f32[8,48,8,128]{3,2,1,0:T(8,128)S(1)} %bitcast.135, s32[128,128]{1,0:T(8,128)S(1)} %bitcast.137, s32[128,128]{1,0:T(8,128)S(1)} %bitcast.138, f32[3,128,128]{2,1,0:T(8,128)S(1)} %bitcast.136), custom_call_target="tpu_custom_call" | custom-call | tf_op jit(solution)/shard_map/pallas_call | solution.py:171
  153.2 0.5 add_dynamic-update-slice_fusion.5
  153.7 0.9 add_dynamic-update-slice_fusion.4
  154.5 0.8 add_dynamic-update-slice_fusion.3
  155.4 0.2 add_dynamic-update-slice_fusion.2
  155.6 0.2 add_dynamic-update-slice_fusion.1
  155.7 0.0 copy-start.6
  155.8 0.7 copy-done.6
  156.5 1.1 add_dynamic-update-slice_fusion
  (1 shorter events, 0.0 us)
Async XLA Ops:
  0.0 39.3 %copy-start = (s32[8,1,4]{0,2,1:T(4,128)S(1)}, s32[8,1,4]{0,2,1:T(4,128)}, u32[]{:S(2)}) copy-start(s32[8,1,4]{0,2,1:T(4,128)} %param.7) | copy-start | bytes 388
  0.0 17.1 %copy-start.5 = (f32[1,1,6,8192]{3,1,2,0:T(1,128)S(1)}, f32[1,1,6,8192]{3,1,2,0:T(1,128)}, u32[]{:S(2)}) copy-start(f32[1,1,6,8192]{3,1,2,0:T(1,128)} %param.6) | copy-start | bytes 589828
  1.2 7.7 %collective-permute-start = (f32[3,64,1,128]{3,2,1,0:T(1,128)S(1)}, f32[3,64,1,128]{3,2,1,0:T(1,128)S(1)}, u32[]{:S(2)}, u32[]{:S(2)}) collective-permute-start(f32[3,64,1,128]{3,2,1,0:T(1,128)S(1)} %get-tuple-element.51), channel_id=1, source_target_pairs={{4,0},{8,4},{12,8},{16,12},{20,16},{24,20},{28,24},{5,1},{9,5},{13... | collective-permute-start | bytes 294920 | tf_op jit(solution)/shard_map/ppermute | solution.py:24
  2.5 36.9 %copy-start.4 = (f32[3,64,2,128]{3,2,1,0:T(2,128)S(1)}, f32[3,64,2,128]{3,2,1,0:T(2,128)}, u32[]{:S(2)}) copy-start(f32[3,64,2,128]{3,2,1,0:T(2,128)} %param.11) | copy-start | bytes 589828
  2.6 8.7 %collective-permute-start.1 = (f32[3,64,1,128]{3,2,1,0:T(1,128)S(1)}, f32[3,64,1,128]{3,2,1,0:T(1,128)S(1)}, u32[]{:S(2)}, u32[]{:S(2)}) collective-permute-start(f32[3,64,1,128]{3,2,1,0:T(1,128)S(1)} %get-tuple-element.50), channel_id=1, source_target_pairs={{0,4},{4,8},{8,12},{12,16},{16,20},{20,24},{24,28},{1,5},{5,9},{9,... | collective-permute-start | bytes 294920 | tf_op jit(solution)/shard_map/ppermute | solution.py:22
  12.7 26.7 %collective-permute-start.2 = (f32[3,64,4,1]{3,2,1,0:T(4,128)S(1)}, f32[3,64,4,1]{3,2,1,0:T(4,128)S(1)}, u32[]{:S(2)}, u32[]{:S(2)}) collective-permute-start(f32[3,64,4,1]{3,2,1,0:T(4,128)S(1)} %get-tuple-element.40), channel_id=1, source_target_pairs={{1,0},{2,1},{3,2},{5,4},{6,5},{7,6},{9,8},{10,9},{11,10},{13,12},{... | collective-permute-start | bytes 9224 | tf_op jit(solution)/shard_map/ppermute | solution.py:24
  14.0 25.4 %collective-permute-start.3 = (f32[3,64,4,1]{3,2,1,0:T(4,128)S(1)}, f32[3,64,4,1]{3,2,1,0:T(4,128)S(1)}, u32[]{:S(2)}, u32[]{:S(2)}) collective-permute-start(f32[3,64,4,1]{3,2,1,0:T(4,128)S(1)} %get-tuple-element.39), channel_id=1, source_target_pairs={{0,1},{1,2},{2,3},{4,5},{5,6},{6,7},{8,9},{9,10},{10,11},{12,13},{... | collective-permute-start | bytes 9224 | tf_op jit(solution)/shard_map/ppermute | solution.py:22
  39.3 18.7 %collective-permute-start.4 = (f32[4,384,128]{2,1,0:T(8,128)S(1)}, f32[4,384,128]{2,1,0:T(8,128)S(1)}, u32[]{:S(2)}, u32[]{:S(2)}) collective-permute-start(f32[4,384,128]{2,1,0:T(8,128)S(1)} %all_gather.3), channel_id=1, source_target_pairs={{0,4},{4,0},{8,12},{12,8},{16,20},{20,16},{24,28},{28,24},{1,5},{5... | collective-permute-start | bytes 2359304 | tf_op jit(solution)/shard_map/ppermute | solution.py:166
  58.2 0.9 copy-start.1
  58.2 0.9 copy-start.2
  58.2 0.9 copy-start.3
  155.7 0.7 copy-start.6
where the time goes:
time: 158 us
  Pallas kernels  94 us (59%)
  blocking collectives  22.2 us (14%)
  waiting for transfers between devices  15.9 us (10%)
  starting transfers between devices  11.3 us (7%)
  other arithmetic  10.7 us (7%)
  local copies, waits for them, and re-layouts  3.37 us (2%)
    pallas_call x1, Pallas kernels, on_device(): pl.pallas_call(sample_kernel, out_shape=jax.ShapeDtypeStruct((groups, 6,...  94 us
    all_gather x1, blocking collectives, on_device(): lax.all_gather(table, 'bx', axis=0, axis_index_groups=[list(range(k, coun...  22.2 us
    ppermute x1, waiting for transfers between devices, on_device(): across = lax.ppermute(line, 'bx', [(i, i ^ 1) for i in range(count)])  12.9 us
    ppermute x2, starting transfers between devices, with_halo(): lax.ppermute(tail, axis, [(i, (i + 1) % count) for i in range(ends)])  8.69 us
  transfers between devices with their start and end apart: 5, of which 3 were waited for; matrix products, arithmetic and copies ran while one was open for 4% of the time, Pallas kernels for 0%

commit v1 on v0

v1 whole, which is shorter than its diff:
```python
import functools

import jax
import jax.numpy as jnp
from jax import lax
from jax.experimental import pallas as pl
from jax.experimental.pallas import tpu as pltpu
from jax.sharding import PartitionSpec as P

PX = 8
PY = 8
PZ = 128
STEPS = 2
PARTS = 6
DENSE = 6
WIDE = 1024
UNROLL = 16
F32 = jnp.float32
BF16 = jnp.bfloat16
VMEM = pl.BlockSpec(memory_space=pltpu.VMEM)
SMEM = pl.BlockSpec(memory_space=pltpu.SMEM)


def kernel_call(body, outs, ins, scratch=(), aliases=None, cost=None):
    return pl.pallas_call(
        body,
        out_shape=outs,
        in_specs=ins,
        out_specs=jax.tree.map(lambda _: VMEM, outs),
        scratch_shapes=list(scratch),
        input_output_aliases=aliases or {},
        cost_estimate=cost,
        compiler_params=pltpu.CompilerParams(vmem_limit_bytes=40 * 2**20),
    )


def rank_kernel(slots, slot_ref, pos_ref, dest_ref, info_ref):
    groups = slot_ref.shape[0]
    row = lax.broadcasted_iota(jnp.int32, (PZ, PZ), 0)
    col = lax.broadcasted_iota(jnp.int32, (PZ, PZ), 1)
    before = jnp.where(row < col, 1.0, 0.0).astype(BF16)
    grow = lax.broadcasted_iota(jnp.int32, (groups, groups), 0)
    gcol = lax.broadcasted_iota(jnp.int32, (groups, groups), 1)
    gbefore = jnp.where(grow < gcol, 1.0, 0.0).astype(BF16)
    gafter = jnp.where(grow > gcol, 1.0, 0.0).astype(BF16)
    ones = jnp.ones((PZ, PZ), BF16)
    dest = jnp.zeros((groups, PZ), F32)
    pos = jnp.zeros((groups, PZ), F32)
    start = jnp.zeros((groups, PZ), F32)
    for s in range(slots):
        on = slot_ref[...] == s
        mask = jnp.where(on, 1.0, 0.0).astype(BF16)
        rank = jnp.dot(mask, before, preferred_element_type=F32)
        count = jnp.dot(mask, ones, preferred_element_type=F32)
        base = jnp.dot(gafter, count.astype(BF16), preferred_element_type=F32)
        dest = jnp.where(on, rank + start, dest)
        pos = jnp.where(on, rank + base, pos)
        start = start + count
        across = lax.dot_general(ones[:PY], mask, (((1,), (1,)), ((), ())), preferred_element_type=F32)
        ahead = jnp.dot(across.astype(BF16), gbefore, preferred_element_type=F32)
        info_ref[s : s + 1, :] = ahead[0:1].astype(jnp.int32)
        info_ref[slots + s : slots + s + 1, :] = across[0:1].astype(jnp.int32)
    pos_ref[...] = pos.astype(jnp.int32)
    dest_ref[...] = dest.astype(jnp.int32)


def sort_kernel(slots, info_ref, dest_ref, cell_ref, frac_ref, sorted_ref, load_ref, index_ref):
    groups = dest_ref.shape[0]
    for b in range(groups // 8):
        here = slice(8 * b, 8 * b + 8)
        cell = cell_ref[here, :]
        rows = [frac_ref[i, here, :] for i in range(3)]
        rows += [(cell // (PY * PZ)).astype(F32), ((cell // PZ) & (PY - 1)).astype(F32), (cell & (PZ - 1)).astype(F32)]
        for i, values in enumerate(rows):
            load_ref[pl.ds(64 * b + i, 8, stride=8), :] = values
    lane = lax.broadcasted_iota(jnp.int32, (8, PZ), 1)
    lanes = lane.astype(F32).astype(BF16)
    place = lax.broadcasted_iota(jnp.int32, (PZ, PZ), 0)

    def invert(b, carry):
        first = pl.multiple_of(b * 8, 8)
        dest = dest_ref[pl.ds(first, 8), :]
        moves = jnp.concatenate(
            [jnp.where(place == dest[j : j + 1, :], 1.0, 0.0).astype(BF16) for j in range(8)], axis=0
        )
        index = lax.dot_general(lanes, moves, (((1,), (1,)), ((), ())), preferred_element_type=F32).astype(jnp.int32)
        for j in range(8):
            index_ref[first + j] = index[:, PZ * j : PZ * j + PZ]
        return carry

    lax.fori_loop(0, groups // 8, invert, 0)

    def append(b, carry):
        rows = []
        for j in range(UNROLL):
            g = b * UNROLL + j
            values = load_ref[pl.ds(pl.multiple_of(g * 8, 8), 8), :]
            ordered = jnp.take_along_axis(values, index_ref[g], axis=1, mode="promise_in_bounds")
            start = 0
            for s in range(slots):
                base = info_ref[s, g]
                offset = base & (PZ - 1)
                rows.append((s, base // PZ, offset, pltpu.roll(ordered, (offset - start) & (PZ - 1), axis=1)))
                start = start + info_ref[slots + s, g]
        for s, at, offset, values in rows:
            pltpu.store(sorted_ref.at[s, at], values, mask=lane >= offset)
            sorted_ref[s, at + 1] = values
        return carry

    lax.fori_loop(0, groups // UNROLL, append, 0)


def fold_rows(values):
    row = lax.broadcasted_iota(jnp.int32, values[0].shape, 0)
    values = list(values) + [jnp.zeros_like(values[0])] * (8 - len(values))
    for step in (1, 2, 4):
        low = (row & step) == 0
        values = [
            jnp.where(low, a, b) + pltpu.roll(jnp.where(low, b, a), step, axis=0)
            for a, b in zip(values[0::2], values[1::2])
        ]
    return values[0]


def sample_slot(s, block_ref, total, sorted_ref, out_ref, table_ref):
    dense = PARTS * PY * DENSE
    width = PY * DENSE
    for c in range(PARTS):
        part = block_ref[c * PX * PY : c * PX * PY + width]
        high = part.astype(BF16)
        low = (part - high.astype(F32)).astype(BF16)
        at = c * width
        for k in range(2):
            table_ref[at : at + width, PZ * k : PZ * k + PZ] = high
            table_ref[dense + at : dense + at + width, PZ * k : PZ * k + PZ] = low
    per = WIDE // PZ
    row = lax.broadcasted_iota(jnp.int32, (PY, PZ), 0).astype(F32)
    depth = lax.broadcasted_iota(jnp.int32, (PZ, WIDE), 0).astype(F32).astype(BF16)

    def in_two(value):
        high = value.astype(BF16).astype(F32)
        return high, value - high

    def packed(value):
        return jnp.broadcast_to(value, (16, WIDE)).astype(BF16)[0:1]

    def step(i, carry):
        loads = [sorted_ref[s, i * per + j] for j in range(per)]
        wide = jnp.concatenate(loads, axis=1)
        along_z, iz = wide[2:3], wide[5:6]
        lower_high, lower_low = in_two(1.0 - along_z)
        upper_high, upper_low = in_two(along_z)
        none = jnp.zeros((), BF16)
        at_lower = depth == packed(iz)
        at_upper = depth == packed(iz + 1.0)
        high = jnp.where(at_lower, packed(lower_high), jnp.where(at_upper, packed(upper_high), none))
        low = jnp.where(at_lower, packed(lower_low), jnp.where(at_upper, packed(upper_low), none))
        product = jnp.dot(table_ref[...], jnp.concatenate([high, low], axis=0), preferred_element_type=F32)
        for j in range(per):
            fx, fy, fz, ix, iy, iz = [jnp.broadcast_to(loads[j][k : k + 1], (PY, PZ)) for k in range(6)]
            lower = jnp.clip(iz.astype(jnp.int32), 0, PZ - 2)
            upper = lower + 1
            weight_y = jnp.where(row == iy, 1.0 - fy, jnp.where(row == iy + 1.0, fy, 0.0))
            lanes = slice(PZ * j, PZ * j + PZ)
            totals = [None] * PARTS
            for x in range(PX):
                weight = weight_y * jnp.where(ix == float(x), 1.0 - fx, jnp.where(ix == float(x - 1), fx, 0.0))
                weight_lower, weight_upper = weight * (1.0 - fz), weight * fz
                for c in range(PARTS):
                    if x < DENSE:
                        at = c * width + x * PY
                        term = (product[at : at + PY, lanes] + product[dense + at : dense + at + PY, lanes]) * weight
                    else:
                        at = (c * PX + x) * PY
                        cells = block_ref[at : at + PY]
                        term = (
                            jnp.take_along_axis(cells, lower, axis=1, mode="promise_in_bounds") * weight_lower
                            + jnp.take_along_axis(cells, upper, axis=1, mode="promise_in_bounds") * weight_upper
                        )
                    totals[c] = term if x == 0 else totals[c] + term
            out_ref[s, i * per + j] = fold_rows(totals)
        return carry

    lax.fori_loop(0, (total + WIDE - 1) // WIDE, step, 0)


def sample_kernel(slots, first, blocks, again, plan_ref, info_ref, sorted_ref, *refs):
    block_refs = refs[:blocks]
    out_ref, table_ref = refs[blocks + again :]
    last = info_ref.shape[1] - 1
    for b in range(blocks):
        s = plan_ref[first + b]

        @pl.when(s >= 0)
        def _():
            total = info_ref[s, last] + info_ref[slots + s, last]
            sample_slot(s, block_refs[b], total, sorted_ref, out_ref, table_ref)


def sample(slots, first, blocks, plan, info, ordered, before):
    again = 0 if before is None else 1
    return kernel_call(
        functools.partial(sample_kernel, slots, first, len(blocks), again),
        jax.ShapeDtypeStruct(ordered.shape, F32),
        [SMEM, SMEM] + [VMEM] * (1 + len(blocks) + again),
        [pltpu.VMEM((2 * PARTS * PY * DENSE, 2 * PZ), BF16)],
        {3 + len(blocks): 0} if again else None,
    )(plan, info, ordered, *blocks, *([before] if again else []))


def transpose_inverse(matrix):
    cof_00 = matrix[1][1] * matrix[2][2] - matrix[1][2] * matrix[2][1]
    cof_01 = -(matrix[1][0] * matrix[2][2] - matrix[1][2] * matrix[2][0])
    cof_02 = matrix[1][0] * matrix[2][1] - matrix[1][1] * matrix[2][0]
    cof_10 = -(matrix[0][1] * matrix[2][2] - matrix[0][2] * matrix[2][1])
    cof_11 = matrix[0][0] * matrix[2][2] - matrix[0][2] * matrix[2][0]
    cof_12 = -(matrix[0][0] * matrix[2][1] - matrix[0][1] * matrix[2][0])
    cof_20 = matrix[0][1] * matrix[1][2] - matrix[0][2] * matrix[1][1]
    cof_21 = -(matrix[0][0] * matrix[1][2] - matrix[0][2] * matrix[1][0])
    cof_22 = matrix[0][0] * matrix[1][1] - matrix[0][1] * matrix[1][0]
    determinant = matrix[0][0] * cof_00 + matrix[0][1] * cof_01 + matrix[0][2] * cof_02
    reciprocal = 1.0 / determinant
    return [
        [cof_00 * reciprocal, cof_01 * reciprocal, cof_02 * reciprocal],
        [cof_10 * reciprocal, cof_11 * reciprocal, cof_12 * reciprocal],
        [cof_20 * reciprocal, cof_21 * reciprocal, cof_22 * reciprocal],
    ]


def polar_factor(jacobian):
    rotation = jacobian
    for repeat in range(STEPS):
        inverse = transpose_inverse(rotation)
        rotation = [
            [0.5 * (rotation[first][second] + inverse[first][second]) for second in range(3)] for first in range(3)
        ]
    return rotation


def reorient(rotation, components):
    tensor = [
        [components[0], components[3], components[4]],
        [components[3], components[1], components[5]],
        [components[4], components[5], components[2]],
    ]
    left = [
        [
            rotation[first][0] * tensor[0][second]
            + rotation[first][1] * tensor[1][second]
            + rotation[first][2] * tensor[2][second]
            for second in range(3)
        ]
        for first in range(3)
    ]

    def entry(first, second):
        return (
            left[first][0] * rotation[second][0]
            + left[first][1] * rotation[second][1]
            + left[first][2] * rotation[second][2]
        )

    return [entry(0, 0), entry(1, 1), entry(2, 2), entry(0, 1), entry(0, 2), entry(1, 2)]


def rotation_kernel(field_ref, left_ref, right_ref, down_ref, up_ref, out_ref, wide_ref, slope_ref, edge_ref):
    rows = field_ref.shape[1]
    edge_ref[...] = jnp.zeros_like(edge_ref)
    edge_ref[0:3, :] = down_ref[...]
    edge_ref[3:6, :] = up_ref[...]
    edges = edge_ref[...].T
    for c in range(3):
        wide_ref[c, 0:8, :] = jnp.zeros((8, PZ), F32)
        wide_ref[c, 8 : 8 + rows, :] = field_ref[c]
        wide_ref[c, 8 + rows : 16 + rows, :] = jnp.zeros((8, PZ), F32)
        even = wide_ref[c, pl.ds(8, rows // 2, stride=2), :]
        odd = wide_ref[c, pl.ds(9, rows // 2, stride=2), :]
        slope_ref[c, pl.ds(0, rows // 2, stride=2), :] = 0.5 * (odd - left_ref[c])
        slope_ref[c, pl.ds(1, rows // 2, stride=2), :] = 0.5 * (right_ref[c] - even)
    lane = lax.broadcasted_iota(jnp.int32, (16, PZ), 1)
    for b in range(rows // 16):
        jacobian = []
        for c in range(3):
            at = 16 * b
            middle = field_ref[c, at : at + 16, :]
            after = pltpu.roll(middle, PZ - 1, axis=1)
            after = jnp.where(lane == PZ - 1, edges[at : at + 16, 3 + c : 4 + c], after)
            prior = pltpu.roll(middle, 1, axis=1)
            prior = jnp.where(lane == 0, edges[at : at + 16, c : c + 1], prior)
            slopes = [
                slope_ref[c, at : at + 16, :],
                0.5 * (after - prior),
                0.5 * (wide_ref[c, at + 10 : at + 26, :] - wide_ref[c, at + 6 : at + 22, :]),
            ]
            jacobian.append([slopes[d] + 1.0 if d == c else slopes[d] for d in range(3)])
        rotation = polar_factor(jacobian)
        for first in range(3):
            for second in range(3):
                out_ref[3 * first + second, at : at + 16, :] = rotation[first][second]


def along(values, axis, pairs):
    return lax.ppermute(values, axis, pairs)


def rotations(displace):
    depth, wide = displace.shape[1], displace.shape[2]
    rows = depth * wide

    def steps(axis):
        return [(i, i + 1) for i in range(lax.axis_size(axis) - 1)]

    def back(pairs):
        return [(b, a) for a, b in pairs]

    left = along(displace[:, :, wide - 1, :], "bx", steps("bx"))
    right = along(displace[:, :, 0, :], "bx", back(steps("bx")))
    down = along(displace[:, :, :, PZ - 1].reshape(3, rows), "by", steps("by"))
    up = along(displace[:, :, :, 0].reshape(3, rows), "by", back(steps("by")))
    return kernel_call(
        rotation_kernel,
        jax.ShapeDtypeStruct((9, rows, PZ), F32),
        [VMEM] * 5,
        [
            pltpu.VMEM((3, rows + 16, PZ), F32),
            pltpu.VMEM((3, rows, PZ), F32),
            pltpu.VMEM((8, rows), F32),
        ],
    )(displace.reshape(3, rows, PZ), left, right, down, up)


def finish_kernel(slots, info_ref, slot_ref, pos_ref, samples_ref, rotation_ref, out_ref, row_ref):
    groups = slot_ref.shape[0]
    lane = lax.broadcasted_iota(jnp.int32, (8, PZ), 1)

    def step(b, carry):
        first = pl.multiple_of(b * UNROLL, UNROLL)
        slot_rows = slot_ref[pl.ds(first, UNROLL), :]
        lane_rows = pos_ref[pl.ds(first, UNROLL), :] & (PZ - 1)
        for j in range(UNROLL):
            slot = jnp.broadcast_to(slot_rows[j : j + 1], (8, PZ))
            index = jnp.broadcast_to(lane_rows[j : j + 1], (8, PZ))
            result = None
            for s in range(slots):
                base = info_ref[s, first + j]
                offset, at = base & (PZ - 1), base // PZ
                both = jnp.where(lane >= offset, samples_ref[s, at], samples_ref[s, at + 1])
                value = jnp.take_along_axis(both, index, axis=1, mode="promise_in_bounds")
                result = value if s == 0 else jnp.where(slot == s, value, result)
            row_ref[pl.ds(pl.multiple_of((first + j) * 8, 8), 8), :] = result
        for k in range(UNROLL // 8):
            at = pl.multiple_of(first + 8 * k, 8)
            components = [row_ref[pl.ds(at * 8 + c, 8, stride=8), :] for c in range(PARTS)]
            rotation = [[rotation_ref[3 * m + n, pl.ds(at, 8), :] for n in range(3)] for m in range(3)]
            for c, value in enumerate(reorient(rotation, components)):
                out_ref[c, pl.ds(at, 8), :] = value
        return carry

    lax.fori_loop(0, groups // UNROLL, step, 0)


def on_device(source, lists, voxel_slot, voxel_cell, frac, displace):
    count = lax.axis_size("bx")
    row = lax.axis_index("bx")
    lines = count // 2
    slots = lists.shape[2]
    voxels = voxel_cell.shape[2]
    groups = voxels // PZ
    table = source.reshape(PARTS * PX * PY, PZ)

    swap = [(i, i ^ 1) for i in range(count)]
    forward = [(i, (i + 2) % count) for i in range(count)]
    backward = [(b, a) for a, b in forward]
    arrivals = [(table, 0, 0), (along(table, "bx", swap), 0, 1)]
    ahead = behind = table
    for k in range(1, lines // 2 + 1):
        ahead = along(ahead, "bx", forward)
        new = [(ahead, k)]
        if k <= (lines - 1) // 2:
            behind = along(behind, "bx", backward)
            new.append((behind, -k))
        arrivals += [(b, k, 0) for b, k in new]
        arrivals += [(along(b, "bx", swap), k, 1) for b, k in new]

    my_slabs = lax.dynamic_index_in_dim(lists[:, 0, :], row, 0, keepdims=False)
    far = jnp.array([k for _, k, _ in arrivals], jnp.int32)
    over = jnp.array([k for _, _, k in arrivals], jnp.int32)
    owners = ((row // 2 - far + count) % lines) * 2 + (row % 2 + over) % 2
    listed = owners[:, None] == my_slabs[None, :]
    plan = jnp.max(jnp.where(listed, jnp.arange(slots, dtype=jnp.int32)[None, :], -1), axis=1)

    slot_rows = voxel_slot.reshape(groups, PZ)
    ints = jax.ShapeDtypeStruct((groups, PZ), jnp.int32)
    pos, dest, info = kernel_call(
        functools.partial(rank_kernel, slots),
        (ints, ints, jax.ShapeDtypeStruct((2 * slots, groups), jnp.int32)),
        [VMEM],
    )(slot_rows)
    ordered = kernel_call(
        functools.partial(sort_kernel, slots),
        jax.ShapeDtypeStruct((slots, groups + WIDE // PZ, 8, PZ), F32),
        [SMEM, VMEM, VMEM, VMEM],
        [pltpu.VMEM((groups * 8, PZ), F32), pltpu.VMEM((groups, 8, PZ), jnp.int32)],
    )(info, dest, voxel_cell.reshape(groups, PZ), frac.reshape(3, groups, PZ))
    rotation = rotations(displace)

    samples = None
    cuts = [0] + [c for c in (2, 4, count - 1, count) if c <= count]
    for first, last in zip(cuts[:-1], cuts[1:]):
        blocks = [b for b, _, _ in arrivals[first:last]]
        samples = sample(slots, first, blocks, plan, info, ordered, samples)

    result = kernel_call(
        functools.partial(finish_kernel, slots),
        jax.ShapeDtypeStruct((PARTS, groups, PZ), F32),
        [SMEM] + [VMEM] * 4,
        [pltpu.VMEM((groups * 8, PZ), F32)],
    )(info, slot_rows, pos, samples, rotation)
    return result.reshape(1, 1, PARTS, voxels)


def solution(mesh):
    return jax.shard_map(
        on_device,
        mesh=mesh,
        in_specs=(
            P("bx", "by", None, None),
            P(None, "by", None),
            P("bx", "by", None),
            P("bx", "by", None),
            P("bx", "by", None, None),
            P(None, None, "bx", "by"),
        ),
        out_specs=P("bx", "by", None, None),
        check_vma=False,
    )
```

time: 158 us -> 60.2 us (0.38)
  Pallas kernels: 94 us -> 26.3 us
  blocking collectives: 22.2 us -> 0 us
  other arithmetic: 10.7 us -> 0.77 us
  waiting for transfers between devices: 15.9 us -> 7.37 us
  starting transfers between devices: 11.3 us -> 19.1 us
  local copies, waits for them, and re-layouts: 3.37 us -> 6.2 us
    pallas_call x1 -> x8, Pallas kernels: 94 us -> 26.3 us  [the longest x4 11.9 us: sample(): kernel_call(functools.partial(sample_kernel, slots, first, len(blocks), a...]
    all_gather x1 -> x0, blocking collectives: 22.2 us -> none  [on_device(): lax.all_gather(table, 'bx', axis=0, axis_index_groups=[list(range(k, coun...]
    ppermute x5 -> x11, waiting for transfers between devices: 15.9 us -> 7.37 us  [along(): return lax.ppermute(values, axis, pairs)]
    ppermute x5 -> x11, starting transfers between devices: 11.3 us -> 19.1 us  [along(): return lax.ppermute(values, axis, pairs)]
    mul x4 -> x0, other arithmetic: 3.2 us -> none  [the longest x1 1.78 us: gradients(): grad_x = 0.5 * (full[:, 1:-1, 2:, 1:-1] - full[:, 1:-1, :-2, 1:-1])]
    concatenate x2 -> x0, other arithmetic: 2.69 us -> none  [with_halo(): jnp.concatenate([lax.ppermute(tail, axis, [(i, (i + 1) % count) for i in...]
    unnamed x5 -> x0, other arithmetic: 2.56 us -> none
  transfers between devices with their start and end apart: 5 -> 11, of which waited for: 3 -> 2; matrix products, arithmetic and copies ran while one was open for 4% -> 7% of each run, Pallas kernels for 0% -> 34%
where the time goes in v1:
time: 60.2 us; the launch traced here: 60 us
  Pallas kernels  26.3 us (44%)
  starting transfers between devices  19.1 us (32%)
  waiting for transfers between devices  7.37 us (12%)
  local copies, waits for them, and re-layouts  6.2 us (10%)
  other arithmetic  0.77 us (1%)
    ppermute x11, starting transfers between devices, along(): return lax.ppermute(values, axis, pairs)  19.1 us
    pallas_call x4, Pallas kernels, sample(): kernel_call(functools.partial(sample_kernel, slots, first, len(blocks), a...  11.9 us
    pallas_call x1, Pallas kernels, on_device(): kernel_call(functools.partial(sort_kernel, slots), jax.ShapeDtypeStruct((...  8.19 us
    ppermute x11, waiting for transfers between devices, along(): return lax.ppermute(values, axis, pairs)  7.37 us
    pallas_call x1, Pallas kernels, on_device(): kernel_call(functools.partial(finish_kernel, slots), jax.ShapeDtypeStruct...  5.12 us
    unnamed x14, local copies, waits for them, and re-layouts  2.82 us
    slice x1, local copies, waits for them, and re-layouts, rotations(): up = along(displace[:, :, :, 0].reshape(3, rows), 'by', back(steps('by')))  1.73 us
  transfers between devices with their start and end apart: 11, of which 2 were waited for; matrix products, arithmetic and copies ran while one was open for 7% of the time, Pallas kernels for 34%

profile of v1, /device:TPU:0, one launch (start us, length us, event | category | flops | bytes accessed | tf_op | source)
XLA Modules:
  0.0 60.0 jit_solution(7830008958118002284)
XLA Ops:
  0.0 0.0 copy-start
  0.0 3.0 %collective-permute-start = (f32[384,128]{1,0:T(8,128)}, f32[384,128]{1,0:T(8,128)S(1)}, u32[]{:S(2)}, u32[]{:S(2)}) collective-permute-start(f32[384,128]{1,0:T(8,128)} %bitcast.15), channel_id=1, source_target_pairs={{0,8},{4,12},{8,16},{12,20},{16,24},{20,28},{24,0},{28,4},{1,9},{5... | collective-permute-start | bytes 589832 | tf_op jit(solution)/shard_map/ppermute | solution.py:303
  3.0 1.5 %collective-permute-start.6 = (f32[384,128]{1,0:T(8,128)}, f32[384,128]{1,0:T(8,128)S(1)}, u32[]{:S(2)}, u32[]{:S(2)}) collective-permute-start(f32[384,128]{1,0:T(8,128)} %bitcast.16), channel_id=1, source_target_pairs={{0,4},{4,0},{8,12},{12,8},{16,20},{20,16},{24,28},{28,24},{1,5},{5... | collective-permute-start | bytes 589832 | tf_op jit(solution)/shard_map/ppermute | solution.py:303
  4.5 2.2 %collective-permute-start.4 = (f32[384,128]{1,0:T(8,128)}, f32[384,128]{1,0:T(8,128)S(1)}, u32[]{:S(2)}, u32[]{:S(2)}) collective-permute-start(f32[384,128]{1,0:T(8,128)} %bitcast.17), channel_id=1, source_target_pairs={{8,0},{12,4},{16,8},{20,12},{24,16},{28,20},{0,24},{4,28},{9,1},{1... | collective-permute-start | bytes 589832 | tf_op jit(solution)/shard_map/ppermute | solution.py:303
  6.8 1.7 %slice_reduce_fusion = (f32[3,64,2]{2,1,0:T(8,128)S(1)}, f32[3,64,2]{2,1,0:T(8,128)S(1)}) fusion(f32[3,64,2,128]{3,2,1,0:T(2,128)} %param.13), kind=kLoop, calls=%fused_computation | loop fusion | bytes 6144 | tf_op jit(solution)/shard_map/slice | solution.py:319
  8.5 0.0 copy-start.4
  8.5 0.1 reshape_squeeze.7
  8.7 1.3 %collective-permute-start.10 = (f32[3,128]{1,0:T(4,128)S(1)}, f32[3,128]{1,0:T(4,128)S(1)}, u32[]{:S(2)}, u32[]{:S(2)}) collective-permute-start(f32[3,128]{1,0:T(4,128)S(1)} %reshape_squeeze.7), channel_id=1, source_target_pairs={{1,0},{2,1},{3,2},{5,4},{6,5},{7,6},{9,8},{10,9},{11,10},{13,12},{... | collective-permute-start | bytes 4616 | tf_op jit(solution)/shard_map/ppermute | solution.py:303
  10.0 0.1 reshape_squeeze.6
  10.1 3.0 %collective-permute-start.9 = (f32[3,128]{1,0:T(4,128)S(1)}, f32[3,128]{1,0:T(4,128)S(1)}, u32[]{:S(2)}, u32[]{:S(2)}) collective-permute-start(f32[3,128]{1,0:T(4,128)S(1)} %reshape_squeeze.6), channel_id=1, source_target_pairs={{0,1},{1,2},{2,3},{4,5},{5,6},{6,7},{8,9},{9,10},{10,11},{12,13},{... | collective-permute-start | bytes 4616 | tf_op jit(solution)/shard_map/ppermute | solution.py:303
  13.2 0.0 collective-permute-done.refs_0_
  13.2 0.1 collective-permute-start.1
  13.2 1.2 %fusion.4 = (f32[3,64,1,128]{3,2,1,0:T(1,128)S(1)}, f32[3,64,1,128]{3,2,1,0:T(1,128)S(1)}) fusion(f32[3,64,2,128]{3,2,1,0:T(2,128)} %param.13), kind=kLoop, calls=%fused_computation.15 | loop fusion | bytes 393216 | tf_op jit(solution)/shard_map/slice | solution.py:317
  14.5 0.0 collective-permute-done.10.up_ref
  14.5 2.3 %collective-permute-start.7 = (f32[3,64,128]{2,1,0:T(8,128)S(1)}, f32[3,64,128]{2,1,0:T(8,128)S(1)}, u32[]{:S(2)}, u32[]{:S(2)}) collective-permute-start(f32[3,64,128]{2,1,0:T(8,128)S(1)} %bitcast.22), channel_id=1, source_target_pairs={{0,4},{4,8},{8,12},{12,16},{16,20},{20,24},{24,28},{1,5},{5,9},{9,... | collective-permute-start | bytes 294920 | tf_op jit(solution)/shard_map/ppermute | solution.py:303
  16.7 0.0 collective-permute-done.9.down_ref
  16.8 3.6 %collective-permute-start.3 = (f32[384,128]{1,0:T(8,128)S(1)}, f32[384,128]{1,0:T(8,128)S(1)}, u32[]{:S(2)}, u32[]{:S(2)}) collective-permute-start(f32[384,128]{1,0:T(8,128)S(1)} %collective-permute-done.refs_0_), channel_id=1, source_target_pairs={{0,4},{4,0},{8,12},{12,8},{16,20},{20,16},{24,28},{28,24},{1,5},{5... | collective-permute-start | bytes 589832 | tf_op jit(solution)/shard_map/ppermute | solution.py:303
  20.4 0.0 collective-permute-done.4.refs_1_
  20.4 0.1 collective-permute-start.5
  20.4 2.2 %collective-permute-done.1.refs_2_ = f32[384,128]{1,0:T(8,128)S(1)} collective-permute-done((f32[384,128]{1,0:T(8,128)S(1)}, f32[384,128]{1,0:T(8,128)S(1)}, u32[]{:S(2)}, u32[]{:S(2)}) %collective-permute-start.1) | collective-permute-done | bytes 196640 | tf_op jit(solution)/shard_map/ppermute | solution.py:303
  22.7 0.7 %collective-permute-start.2 = (f32[384,128]{1,0:T(8,128)S(1)}, f32[384,128]{1,0:T(8,128)S(1)}, u32[]{:S(2)}, u32[]{:S(2)}) collective-permute-start(f32[384,128]{1,0:T(8,128)S(1)} %collective-permute-done.1.refs_2_), channel_id=1, source_target_pairs={{0,4},{4,0},{8,12},{12,8},{16,20},{20,16},{24,28},{28,24},{1,5},{5... | collective-permute-start | bytes 589832 | tf_op jit(solution)/shard_map/ppermute | solution.py:303
  23.3 0.7 %fusion = s32[8]{0:T(128)S(1)} fusion(s32[8]{0:T(128)} %constant.65.clone, s32[8]{0:T(128)} %constant.72, s32[]{:T(128)S(6)} %select_n.31, s32[]{:T(128)S(6)} %select_n.29), kind=kLoop, calls=%fused_computation.10 | loop fusion | flops 216 | bytes 104 | tf_op jit(solution)/shard_map/add | solution.py:388
  24.0 0.0 copy-start.2
  24.0 0.8 %copy-done.2 = s32[1,1,16384]{2,1,0:T(1,128)S(1)} copy-done((s32[1,1,16384]{2,1,0:T(1,128)S(1)}, s32[1,1,16384]{2,1,0:T(1,128)}, u32[]{:S(2)}) %copy-start.2) | copy-done | bytes 65560
  24.9 0.5 shard_map.82
  25.3 0.0 copy-done
  25.3 0.2 dynamic-slice_reduce_fusion
  25.5 0.9 %copy-done.5 = f32[1,1,3,16384]{3,1,2,0:T(1,128)S(1)} copy-done((f32[1,1,3,16384]{3,1,2,0:T(1,128)S(1)}, f32[1,1,3,16384]{3,1,2,0:T(1,128)}, u32[]{:S(2)}) %copy-start.5) | copy-done | bytes 196632
  26.4 0.8 %copy-done.6 = s32[1,1,16384]{2,1,0:T(1,128)S(1)} copy-done((s32[1,1,16384]{2,1,0:T(1,128)S(1)}, s32[1,1,16384]{2,1,0:T(1,128)}, u32[]{:S(2)}) %copy-start.6) | copy-done | bytes 65560
  27.3 8.2 %shard_map.83.sorted_ref = f32[4,136,8,128]{3,2,1,0:T(8,128)S(1)} custom-call(s32[8,128]{1,0:T(8,128)S(1)} %get-tuple-element.8.info_ref, s32[128,128]{1,0:T(8,128)S(1)} %get-tuple-element.10.dest_ref, s32[128,128]{1,0:T(8,128)S(1)} %bitcast.20, f32[3,128,128]{2,1,0:T(8,128)S(1)} %bitcast.19), custom_call_target="tpu_custom_call" | custom-call | tf_op jit(solution)/shard_map/pallas_call | solution.py:399
  35.5 0.0 collective-permute-done.7.left_ref
  35.5 1.3 %collective-permute-start.8 = (f32[3,64,128]{2,1,0:T(8,128)S(1)}, f32[3,64,128]{2,1,0:T(8,128)S(1)}, u32[]{:S(2)}, u32[]{:S(2)}) collective-permute-start(f32[3,64,128]{2,1,0:T(8,128)S(1)} %bitcast.21), channel_id=1, source_target_pairs={{4,0},{8,4},{12,8},{16,12},{20,16},{24,20},{28,24},{5,1},{9,5},{13... | collective-permute-start | bytes 294920 | tf_op jit(solution)/shard_map/ppermute | solution.py:303
  36.8 0.1 select_reduce_fusion.plan_ref
  36.9 5.1 %collective-permute-done.8.right_ref = f32[3,64,128]{2,1,0:T(8,128)S(1)} collective-permute-done((f32[3,64,128]{2,1,0:T(8,128)S(1)}, f32[3,64,128]{2,1,0:T(8,128)S(1)}, u32[]{:S(2)}, u32[]{:S(2)}) %collective-permute-start.8) | collective-permute-done | bytes 98336 | tf_op jit(solution)/shard_map/ppermute | solution.py:303
  42.0 0.0 copy-done.1
  42.0 0.6 %shard_map.88.rotation_ref = f32[9,128,128]{2,1,0:T(8,128)S(1)} custom-call(f32[3,128,128]{2,1,0:T(8,128)S(1)} %bitcast.12, f32[3,64,128]{2,1,0:T(8,128)S(1)} %collective-permute-done.7.left_ref, f32[3,64,128]{2,1,0:T(8,128)S(1)} %collective-permute-done.8.right_ref, f32[3,128]{1,0:T(4,128)S(1)} %collective-permute-done.9.down_ref, ...), custom_call_target="tpu_custom_call" | custom-call | tf_op jit(solution)/shard_map/pallas_call | solution.py:320
  42.6 0.0 collective-permute-done.6.refs_1_
  42.7 0.0 copy-done.4
  42.7 2.7 %shard_map.84.refs_2_ = f32[4,136,8,128]{3,2,1,0:T(8,128)S(1)} custom-call(s32[8]{0:T(128)S(1)} %select_reduce_fusion.plan_ref, s32[8,128]{1,0:T(8,128)S(1)} %get-tuple-element.8.info_ref, f32[4,136,8,128]{3,2,1,0:T(8,128)S(1)} %shard_map.83.sorted_ref, f32[384,128]{1,0:T(8,128)S(1)} %bitcast.18, f32[384,128]{1,0:T(8,128)S(1)} %collective-permute-done.6.refs_1_), custom_call_target="tpu_custom_call" | custom-call | tf_op jit(solution)/shard_map/pallas_call | solution.py:202
  45.4 3.2 %shard_map.85.refs_3_ = f32[4,136,8,128]{3,2,1,0:T(8,128)S(1)} custom-call(s32[8]{0:T(128)S(1)} %select_reduce_fusion.plan_ref, s32[8,128]{1,0:T(8,128)S(1)} %get-tuple-element.8.info_ref, f32[4,136,8,128]{3,2,1,0:T(8,128)S(1)} %shard_map.83.sorted_ref, f32[384,128]{1,0:T(8,128)S(1)} %collective-permute-done.refs_0_, ...), custom_call_target="tpu_custom_call", output_to_operand_aliasing={{}: (5, {})} | custom-call | tf_op jit(solution)/shard_map/pallas_call | solution.py:202
  48.7 0.0 collective-permute-done.3.refs_0_
  48.7 0.0 collective-permute-done.5.refs_1_
  48.7 5.4 %shard_map.86.refs_1_ = f32[4,136,8,128]{3,2,1,0:T(8,128)S(1)} custom-call(s32[8]{0:T(128)S(1)} %select_reduce_fusion.plan_ref, s32[8,128]{1,0:T(8,128)S(1)} %get-tuple-element.8.info_ref, f32[4,136,8,128]{3,2,1,0:T(8,128)S(1)} %shard_map.83.sorted_ref, f32[384,128]{1,0:T(8,128)S(1)} %collective-permute-done.3.refs_0_, ...), custom_call_target="tpu_custom_call", output_to_operand_aliasing={{}: (6, {})} | custom-call | tf_op jit(solution)/shard_map/pallas_call | solution.py:202
  54.0 0.0 copy-start.3
  54.1 0.0 collective-permute-done.2.refs_0_
  54.1 0.6 %shard_map.87.samples_ref = f32[4,136,8,128]{3,2,1,0:T(8,128)S(1)} custom-call(s32[8]{0:T(128)S(1)} %select_reduce_fusion.plan_ref, s32[8,128]{1,0:T(8,128)S(1)} %get-tuple-element.8.info_ref, f32[4,136,8,128]{3,2,1,0:T(8,128)S(1)} %shard_map.83.sorted_ref, f32[384,128]{1,0:T(8,128)S(1)} %collective-permute-done.2.refs_0_, ...), custom_call_target="tpu_custom_call", output_to_operand_aliasing={{}: (4, {})} | custom-call | tf_op jit(solution)/shard_map/pallas_call | solution.py:202
  54.7 0.2 copy-done.3
  54.9 5.1 %shard_map.89 = f32[6,128,128]{2,1,0:T(8,128)} custom-call(s32[8,128]{1,0:T(8,128)S(1)} %get-tuple-element.8.info_ref, s32[128,128]{1,0:T(8,128)S(1)} %bitcast.14, s32[128,128]{1,0:T(8,128)S(1)} %get-tuple-element.9.pos_ref, f32[4,136,8,128]{3,2,1,0:T(8,128)S(1)} %shard_map.87.samples_ref, f32[9,128,128]{2,1,0:T(8,128)S(1)} %shard_map.88.rotation_ref), custom_call_target="tpu_custom_call" | custom-call | tf_op jit(solution)/shard_map/pallas_call | solution.py:413
  (3 shorter events, 0.0 us)
Async XLA Ops:
  0.0 25.3 %copy-start = (s32[8,1,4]{0,2,1:T(4,128)S(1)}, s32[8,1,4]{0,2,1:T(4,128)}, u32[]{:S(2)}) copy-start(s32[8,1,4]{0,2,1:T(4,128)} %param.9) | copy-start | bytes 388
  0.0 42.0 %copy-start.1 = (f32[3,64,2,128]{3,2,1,0:T(2,128)S(1)}, f32[3,64,2,128]{3,2,1,0:T(2,128)}, u32[]{:S(2)}) copy-start(f32[3,64,2,128]{3,2,1,0:T(2,128)} %param.13) | copy-start | bytes 589828
  0.0 13.2 %collective-permute-start = (f32[384,128]{1,0:T(8,128)}, f32[384,128]{1,0:T(8,128)S(1)}, u32[]{:S(2)}, u32[]{:S(2)}) collective-permute-start(f32[384,128]{1,0:T(8,128)} %bitcast.15), channel_id=1, source_target_pairs={{0,8},{4,12},{8,16},{12,20},{16,24},{20,28},{24,0},{28,4},{1,9},{5... | collective-permute-start | bytes 589832 | tf_op jit(solution)/shard_map/ppermute | solution.py:303
  3.0 39.6 %collective-permute-start.6 = (f32[384,128]{1,0:T(8,128)}, f32[384,128]{1,0:T(8,128)S(1)}, u32[]{:S(2)}, u32[]{:S(2)}) collective-permute-start(f32[384,128]{1,0:T(8,128)} %bitcast.16), channel_id=1, source_target_pairs={{0,4},{4,0},{8,12},{12,8},{16,20},{20,16},{24,28},{28,24},{1,5},{5... | collective-permute-start | bytes 589832 | tf_op jit(solution)/shard_map/ppermute | solution.py:303
  4.5 15.8 %collective-permute-start.4 = (f32[384,128]{1,0:T(8,128)}, f32[384,128]{1,0:T(8,128)S(1)}, u32[]{:S(2)}, u32[]{:S(2)}) collective-permute-start(f32[384,128]{1,0:T(8,128)} %bitcast.17), channel_id=1, source_target_pairs={{8,0},{12,4},{16,8},{20,12},{24,16},{28,20},{0,24},{4,28},{9,1},{1... | collective-permute-start | bytes 589832 | tf_op jit(solution)/shard_map/ppermute | solution.py:303
  8.5 34.1 %copy-start.4 = (f32[1,1,6,8192]{3,1,2,0:T(1,128)S(1)}, f32[1,1,6,8192]{3,1,2,0:T(1,128)}, u32[]{:S(2)}) copy-start(f32[1,1,6,8192]{3,1,2,0:T(1,128)} %param.8) | copy-start | bytes 589828
  8.7 5.8 %collective-permute-start.10 = (f32[3,128]{1,0:T(4,128)S(1)}, f32[3,128]{1,0:T(4,128)S(1)}, u32[]{:S(2)}, u32[]{:S(2)}) collective-permute-start(f32[3,128]{1,0:T(4,128)S(1)} %reshape_squeeze.7), channel_id=1, source_target_pairs={{1,0},{2,1},{3,2},{5,4},{6,5},{7,6},{9,8},{10,9},{11,10},{13,12},{... | collective-permute-start | bytes 4616 | tf_op jit(solution)/shard_map/ppermute | solution.py:303
  10.1 6.6 %collective-permute-start.9 = (f32[3,128]{1,0:T(4,128)S(1)}, f32[3,128]{1,0:T(4,128)S(1)}, u32[]{:S(2)}, u32[]{:S(2)}) collective-permute-start(f32[3,128]{1,0:T(4,128)S(1)} %reshape_squeeze.6), channel_id=1, source_target_pairs={{0,1},{1,2},{2,3},{4,5},{5,6},{6,7},{8,9},{9,10},{10,11},{12,13},{... | collective-permute-start | bytes 4616 | tf_op jit(solution)/shard_map/ppermute | solution.py:303
  13.2 9.5 %collective-permute-start.1 = (f32[384,128]{1,0:T(8,128)S(1)}, f32[384,128]{1,0:T(8,128)S(1)}, u32[]{:S(2)}, u32[]{:S(2)}) collective-permute-start(f32[384,128]{1,0:T(8,128)S(1)} %collective-permute-done.refs_0_), channel_id=1, source_target_pairs={{0,8},{4,12},{8,16},{12,20},{16,24},{20,28},{24,0},{28,4},{1,9},{5... | collective-permute-start | bytes 589832 | tf_op jit(solution)/shard_map/ppermute | solution.py:303
  14.5 21.0 %collective-permute-start.7 = (f32[3,64,128]{2,1,0:T(8,128)S(1)}, f32[3,64,128]{2,1,0:T(8,128)S(1)}, u32[]{:S(2)}, u32[]{:S(2)}) collective-permute-start(f32[3,64,128]{2,1,0:T(8,128)S(1)} %bitcast.22), channel_id=1, source_target_pairs={{0,4},{4,8},{8,12},{12,16},{16,20},{20,24},{24,28},{1,5},{5,9},{9,... | collective-permute-start | bytes 294920 | tf_op jit(solution)/shard_map/ppermute | solution.py:303
  16.8 31.9 %collective-permute-start.3 = (f32[384,128]{1,0:T(8,128)S(1)}, f32[384,128]{1,0:T(8,128)S(1)}, u32[]{:S(2)}, u32[]{:S(2)}) collective-permute-start(f32[384,128]{1,0:T(8,128)S(1)} %collective-permute-done.refs_0_), channel_id=1, source_target_pairs={{0,4},{4,0},{8,12},{12,8},{16,20},{20,16},{24,28},{28,24},{1,5},{5... | collective-permute-start | bytes 589832 | tf_op jit(solution)/shard_map/ppermute | solution.py:303
  20.4 28.3 %collective-permute-start.5 = (f32[384,128]{1,0:T(8,128)S(1)}, f32[384,128]{1,0:T(8,128)S(1)}, u32[]{:S(2)}, u32[]{:S(2)}) collective-permute-start(f32[384,128]{1,0:T(8,128)S(1)} %collective-permute-done.4.refs_1_), channel_id=1, source_target_pairs={{0,4},{4,0},{8,12},{12,8},{16,20},{20,16},{24,28},{28,24},{1,5},{5... | collective-permute-start | bytes 589832 | tf_op jit(solution)/shard_map/ppermute | solution.py:303
  22.7 31.4 %collective-permute-start.2 = (f32[384,128]{1,0:T(8,128)S(1)}, f32[384,128]{1,0:T(8,128)S(1)}, u32[]{:S(2)}, u32[]{:S(2)}) collective-permute-start(f32[384,128]{1,0:T(8,128)S(1)} %collective-permute-done.1.refs_2_), channel_id=1, source_target_pairs={{0,4},{4,0},{8,12},{12,8},{16,20},{20,16},{24,28},{28,24},{1,5},{5... | collective-permute-start | bytes 589832 | tf_op jit(solution)/shard_map/ppermute | solution.py:303
  24.0 0.8 %copy-start.2 = (s32[1,1,16384]{2,1,0:T(1,128)S(1)}, s32[1,1,16384]{2,1,0:T(1,128)}, u32[]{:S(2)}) copy-start(s32[1,1,16384]{2,1,0:T(1,128)} %param.10) | copy-start | bytes 196612
  25.5 0.9 %copy-start.5 = (f32[1,1,3,16384]{3,1,2,0:T(1,128)S(1)}, f32[1,1,3,16384]{3,1,2,0:T(1,128)}, u32[]{:S(2)}) copy-start(f32[1,1,3,16384]{3,1,2,0:T(1,128)} %param.12) | copy-start | bytes 589828
  26.4 0.8 %copy-start.6 = (s32[1,1,16384]{2,1,0:T(1,128)S(1)}, s32[1,1,16384]{2,1,0:T(1,128)}, u32[]{:S(2)}) copy-start(s32[1,1,16384]{2,1,0:T(1,128)} %param.11) | copy-start | bytes 196612
  35.5 6.5 %collective-permute-start.8 = (f32[3,64,128]{2,1,0:T(8,128)S(1)}, f32[3,64,128]{2,1,0:T(8,128)S(1)}, u32[]{:S(2)}, u32[]{:S(2)}) collective-permute-start(f32[3,64,128]{2,1,0:T(8,128)S(1)} %bitcast.21), channel_id=1, source_target_pairs={{4,0},{8,4},{12,8},{16,12},{20,16},{24,20},{28,24},{5,1},{9,5},{13... | collective-permute-start | bytes 294920 | tf_op jit(solution)/shard_map/ppermute | solution.py:303
  54.0 0.8 %copy-start.3 = (s32[1,1,16384]{2,1,0:T(1,128)S(1)}, s32[1,1,16384]{2,1,0:T(1,128)}, u32[]{:S(2)}) copy-start(s32[1,1,16384]{2,1,0:T(1,128)} %param.10) | copy-start | bytes 196612

commit v2 on v1

--- a/solution.py
+++ b/solution.py
@@ -15,27 +15,29 @@
 DENSE = 6
 WIDE = 1024
 UNROLL = 16
+SHARE = 32
 F32 = jnp.float32
 BF16 = jnp.bfloat16
 VMEM = pl.BlockSpec(memory_space=pltpu.VMEM)
 SMEM = pl.BlockSpec(memory_space=pltpu.SMEM)
-
-
-def kernel_call(body, outs, ins, scratch=(), aliases=None, cost=None):
+HBM = pl.BlockSpec(memory_space=pltpu.HBM)
+
+
+def kernel_call(body, outs, ins, scratch=(), aliases=None, cost=1.0, out_spec=VMEM):
     return pl.pallas_call(
         body,
         out_shape=outs,
         in_specs=ins,
-        out_specs=jax.tree.map(lambda _: VMEM, outs),
+        out_specs=jax.tree.map(lambda _: out_spec, outs),
         scratch_shapes=list(scratch),
         input_output_aliases=aliases or {},
-        cost_estimate=cost,
-        compiler_params=pltpu.CompilerParams(vmem_limit_bytes=40 * 2**20),
+        cost_estimate=pl.CostEstimate(flops=0, bytes_accessed=int(cost * 3.0e6), transcendentals=0),
+        compiler_params=pltpu.CompilerParams(vmem_limit_bytes=24 * 2**20),
     )
 
 
-def rank_kernel(slots, slot_ref, pos_ref, dest_ref, info_ref):
-    groups = slot_ref.shape[0]
+def ranks(slots, slot, pos_ref, dest_ref, info_ref):
+    groups = slot.shape[0]
     row = lax.broadcasted_iota(jnp.int32, (PZ, PZ), 0)
     col = lax.broadcasted_iota(jnp.int32, (PZ, PZ), 1)
     before = jnp.where(row < col, 1.0, 0.0).astype(BF16)
@@ -48,7 +50,7 @@
     pos = jnp.zeros((groups, PZ), F32)
     start = jnp.zeros((groups, PZ), F32)
     for s in range(slots):
-        on = slot_ref[...] == s
+        on = slot == s
         mask = jnp.where(on, 1.0, 0.0).astype(BF16)
         rank = jnp.dot(mask, before, preferred_element_type=F32)
         count = jnp.dot(mask, ones, preferred_element_type=F32)
@@ -64,31 +66,48 @@
     dest_ref[...] = dest.astype(jnp.int32)
 
 
-def sort_kernel(slots, info_ref, dest_ref, cell_ref, frac_ref, sorted_ref, load_ref, index_ref):
-    groups = dest_ref.shape[0]
+def order_kernel(
+    slots, slot_hbm, cell_hbm, frac_hbm, sorted_ref, pos_ref, info_ref,
+    slot_ref, cell_ref, frac_ref, dest_ref, load_ref, index_ref, table_ref, sems,
+):
+    groups = pos_ref.shape[0]
+    loads = [
+        pltpu.make_async_copy(slot_hbm, slot_ref, sems.at[0]),
+        pltpu.make_async_copy(cell_hbm, cell_ref, sems.at[1]),
+        pltpu.make_async_copy(frac_hbm, frac_ref, sems.at[2]),
+    ]
+    for load in loads:
+        load.start()
+    loads[0].wait()
+    ranks(slots, slot_ref[...], pos_ref, dest_ref, info_ref)
+    scalars = pltpu.make_async_copy(info_ref, table_ref, sems.at[3])
+    scalars.start()
+    lane = lax.broadcasted_iota(jnp.int32, (8, PZ), 1)
+    lanes = lane.astype(F32).astype(BF16)
+    place = lax.broadcasted_iota(jnp.int32, (PZ, PZ), 0)
+
+    def invert(b, carry):
+        first = pl.multiple_of(b * UNROLL, UNROLL)
+        dest = dest_ref[pl.ds(first, UNROLL), :]
+        moves = jnp.concatenate(
+            [jnp.where(place == dest[j : j + 1, :], 1.0, 0.0).astype(BF16) for j in range(UNROLL)], axis=0
+        )
+        index = lax.dot_general(lanes, moves, (((1,), (1,)), ((), ())), preferred_element_type=F32).astype(jnp.int32)
+        for j in range(UNROLL):
+            index_ref[first + j] = index[:, PZ * j : PZ * j + PZ]
+        return carry
+
+    lax.fori_loop(0, groups // UNROLL, invert, 0)
+    loads[1].wait()
+    loads[2].wait()
     for b in range(groups // 8):
         here = slice(8 * b, 8 * b + 8)
         cell = cell_ref[here, :]
         rows = [frac_ref[i, here, :] for i in range(3)]
-        rows += [(cell // (PY * PZ)).astype(F32), ((cell // PZ) & (PY - 1)).astype(F32), (cell & (PZ - 1)).astype(F32)]
+        rows += [(cell >> 10).astype(F32), ((cell >> 7) & (PY - 1)).astype(F32), (cell & (PZ - 1)).astype(F32)]
         for i, values in enumerate(rows):
             load_ref[pl.ds(64 * b + i, 8, stride=8), :] = values
-    lane = lax.broadcasted_iota(jnp.int32, (8, PZ), 1)
-    lanes = lane.astype(F32).astype(BF16)
-    place = lax.broadcasted_iota(jnp.int32, (PZ, PZ), 0)
-
-    def invert(b, carry):
-        first = pl.multiple_of(b * 8, 8)
-        dest = dest_ref[pl.ds(first, 8), :]
-        moves = jnp.concatenate(
-            [jnp.where(place == dest[j : j + 1, :], 1.0, 0.0).astype(BF16) for j in range(8)], axis=0
-        )
-        index = lax.dot_general(lanes, moves, (((1,), (1,)), ((), ())), preferred_element_type=F32).astype(jnp.int32)
-        for j in range(8):
-            index_ref[first + j] = index[:, PZ * j : PZ * j + PZ]
-        return carry
-
-    lax.fori_loop(0, groups // 8, invert, 0)
+    scalars.wait()
 
     def append(b, carry):
         rows = []
@@ -98,10 +117,10 @@
             ordered = jnp.take_along_axis(values, index_ref[g], axis=1, mode="promise_in_bounds")
             start = 0
             for s in range(slots):
-                base = info_ref[s, g]
+                base = table_ref[s, g]
                 offset = base & (PZ - 1)
-                rows.append((s, base // PZ, offset, pltpu.roll(ordered, (offset - start) & (PZ - 1), axis=1)))
-                start = start + info_ref[slots + s, g]
+                rows.append((s, base >> 7, offset, pltpu.roll(ordered, (offset - start) & (PZ - 1), axis=1)))
+                start = start + table_ref[slots + s, g]
         for s, at, offset, values in rows:
             pltpu.store(sorted_ref.at[s, at], values, mask=lane >= offset)
             sorted_ref[s, at + 1] = values
@@ -205,6 +224,7 @@
         [SMEM, SMEM] + [VMEM] * (1 + len(blocks) + again),
         [pltpu.VMEM((2 * PARTS * PY * DENSE, 2 * PZ), BF16)],
         {3 + len(blocks): 0} if again else None,
+        cost=2.5 * min(slots, len(blocks)),
     )(plan, info, ordered, *blocks, *([before] if again else []))
 
 
@@ -263,8 +283,26 @@
     return [entry(0, 0), entry(1, 1), entry(2, 2), entry(0, 1), entry(0, 2), entry(1, 2)]
 
 
-def rotation_kernel(field_ref, left_ref, right_ref, down_ref, up_ref, out_ref, wide_ref, slope_ref, edge_ref):
+def pack_kernel(odd_ref, table_ref, field_ref, swap_ref, cross_ref, first_ref, last_ref):
+    odd = odd_ref[0] == 1
+    cells = table_ref.shape[0]
+    half = field_ref.shape[1] // 2
+    swap_ref[0:cells, :] = table_ref[...]
+    for c in range(3):
+        even_rows = field_ref[c, pl.ds(0, half, stride=2), :]
+        odd_rows = field_ref[c, pl.ds(1, half, stride=2), :]
+        swap_ref[cells + half * c : cells + half * c + half, :] = jnp.where(odd, even_rows, odd_rows)
+        cross_ref[half * c : half * c + half, :] = jnp.where(odd, odd_rows, even_rows)
+        turned = field_ref[c].T
+        first_ref[c : c + 1, :] = turned[0:1]
+        last_ref[c : c + 1, :] = turned[PZ - 1 : PZ]
+
+
+def rotation_kernel(odd_ref, field_ref, swapped_ref, crossed_ref, down_ref, up_ref, out_ref, wide_ref, slope_ref, edge_ref):
+    odd = odd_ref[0] == 1
     rows = field_ref.shape[1]
+    half = rows // 2
+    cells = swapped_ref.shape[0] - 3 * half
     edge_ref[...] = jnp.zeros_like(edge_ref)
     edge_ref[0:3, :] = down_ref[...]
     edge_ref[3:6, :] = up_ref[...]
@@ -273,10 +311,12 @@
         wide_ref[c, 0:8, :] = jnp.zeros((8, PZ), F32)
         wide_ref[c, 8 : 8 + rows, :] = field_ref[c]
         wide_ref[c, 8 + rows : 16 + rows, :] = jnp.zeros((8, PZ), F32)
-        even = wide_ref[c, pl.ds(8, rows // 2, stride=2), :]
-        odd = wide_ref[c, pl.ds(9, rows // 2, stride=2), :]
-        slope_ref[c, pl.ds(0, rows // 2, stride=2), :] = 0.5 * (odd - left_ref[c])
-        slope_ref[c, pl.ds(1, rows // 2, stride=2), :] = 0.5 * (right_ref[c] - even)
+        even_rows = wide_ref[c, pl.ds(8, half, stride=2), :]
+        odd_rows = wide_ref[c, pl.ds(9, half, stride=2), :]
+        paired = swapped_ref[cells + half * c : cells + half * c + half, :]
+        other = crossed_ref[half * c : half * c + half, :]
+        slope_ref[c, pl.ds(0, half, stride=2), :] = 0.5 * (odd_rows - jnp.where(odd, paired, other))
+        slope_ref[c, pl.ds(1, half, stride=2), :] = 0.5 * (jnp.where(odd, other, paired) - even_rows)
     lane = lax.broadcasted_iota(jnp.int32, (16, PZ), 1)
     for b in range(rows // 16):
         jacobian = []
@@ -303,118 +343,143 @@
     return lax.ppermute(values, axis, pairs)
 
 
-def rotations(displace):
-    depth, wide = displace.shape[1], displace.shape[2]
-    rows = depth * wide
-
-    def steps(axis):
-        return [(i, i + 1) for i in range(lax.axis_size(axis) - 1)]
-
-    def back(pairs):
-        return [(b, a) for a, b in pairs]
-
-    left = along(displace[:, :, wide - 1, :], "bx", steps("bx"))
-    right = along(displace[:, :, 0, :], "bx", back(steps("bx")))
-    down = along(displace[:, :, :, PZ - 1].reshape(3, rows), "by", steps("by"))
-    up = along(displace[:, :, :, 0].reshape(3, rows), "by", back(steps("by")))
-    return kernel_call(
-        rotation_kernel,
-        jax.ShapeDtypeStruct((9, rows, PZ), F32),
-        [VMEM] * 5,
-        [
-            pltpu.VMEM((3, rows + 16, PZ), F32),
-            pltpu.VMEM((3, rows, PZ), F32),
-            pltpu.VMEM((8, rows), F32),
-        ],
-    )(displace.reshape(3, rows, PZ), left, right, down, up)
-
-
-def finish_kernel(slots, info_ref, slot_ref, pos_ref, samples_ref, rotation_ref, out_ref, row_ref):
+def both_ways(pairs):
+    return list(pairs) + [(b, a) for a, b in pairs]
+
+
+def finish_kernel(slots, info_ref, slot_ref, pos_ref, samples_ref, rotation_ref, out_hbm, row_ref, out_ref, sems):
     groups = slot_ref.shape[0]
     lane = lax.broadcasted_iota(jnp.int32, (8, PZ), 1)
-
-    def step(b, carry):
-        first = pl.multiple_of(b * UNROLL, UNROLL)
-        slot_rows = slot_ref[pl.ds(first, UNROLL), :]
-        lane_rows = pos_ref[pl.ds(first, UNROLL), :] & (PZ - 1)
-        for j in range(UNROLL):
-            slot = jnp.broadcast_to(slot_rows[j : j + 1], (8, PZ))
-            index = jnp.broadcast_to(lane_rows[j : j + 1], (8, PZ))
+    stores = []
+    for part in range(groups // SHARE):
+        for g in range(part * SHARE, part * SHARE + SHARE):
+            slot = jnp.broadcast_to(slot_ref[g : g + 1, :], (8, PZ))
+            index = jnp.broadcast_to(pos_ref[g : g + 1, :], (8, PZ)) & (PZ - 1)
             result = None
             for s in range(slots):
-                base = info_ref[s, first + j]
-                offset, at = base & (PZ - 1), base // PZ
+                base = info_ref[s, g]
+                offset, at = base & (PZ - 1), base >> 7
                 both = jnp.where(lane >= offset, samples_ref[s, at], samples_ref[s, at + 1])
                 value = jnp.take_along_axis(both, index, axis=1, mode="promise_in_bounds")
                 result = value if s == 0 else jnp.where(slot == s, value, result)
-            row_ref[pl.ds(pl.multiple_of((first + j) * 8, 8), 8), :] = result
-        for k in range(UNROLL // 8):
-            at = pl.multiple_of(first + 8 * k, 8)
+            row_ref[8 * g : 8 * g + 8, :] = result
+        for at in range(part * SHARE, part * SHARE + SHARE, 8):
             components = [row_ref[pl.ds(at * 8 + c, 8, stride=8), :] for c in range(PARTS)]
-            rotation = [[rotation_ref[3 * m + n, pl.ds(at, 8), :] for n in range(3)] for m in range(3)]
+            rotation = [[rotation_ref[3 * m + n, at : at + 8, :] for n in range(3)] for m in range(3)]
             for c, value in enumerate(reorient(rotation, components)):
-                out_ref[c, pl.ds(at, 8), :] = value
-        return carry
-
-    lax.fori_loop(0, groups // UNROLL, step, 0)
+                out_ref[c, at : at + 8, :] = value
+        here = pl.ds(part * SHARE, SHARE)
+        stores.append(pltpu.make_async_copy(out_ref.at[:, here], out_hbm.at[:, here], sems.at[part]))
+        stores[-1].start()
+    for store in stores:
+        store.wait()
 
 
 def on_device(source, lists, voxel_slot, voxel_cell, frac, displace):
     count = lax.axis_size("bx")
+    columns = lax.axis_size("by")
     row = lax.axis_index("bx")
     lines = count // 2
     slots = lists.shape[2]
     voxels = voxel_cell.shape[2]
     groups = voxels // PZ
-    table = source.reshape(PARTS * PX * PY, PZ)
+    half = groups // 2
+    cells = PARTS * PX * PY
+    table = source.reshape(cells, PZ)
+    field = displace.reshape(3, groups, PZ)
+    odd = (row % 2).astype(jnp.int32).reshape(1)
 
     swap = [(i, i ^ 1) for i in range(count)]
     forward = [(i, (i + 2) % count) for i in range(count)]
     backward = [(b, a) for a, b in forward]
-    arrivals = [(table, 0, 0), (along(table, "bx", swap), 0, 1)]
-    ahead = behind = table
-    for k in range(1, lines // 2 + 1):
-        ahead = along(ahead, "bx", forward)
-        new = [(ahead, k)]
-        if k <= (lines - 1) // 2:
-            behind = along(behind, "bx", backward)
-            new.append((behind, -k))
-        arrivals += [(b, k, 0) for b, k in new]
-        arrivals += [(along(b, "bx", swap), k, 1) for b, k in new]
-
+    line = jax.ShapeDtypeStruct((3, groups), F32)
+    packed, facing, first_lane, last_lane = kernel_call(
+        pack_kernel,
+        (
+            jax.ShapeDtypeStruct((cells + 3 * half, PZ), F32),
+            jax.ShapeDtypeStruct((3 * half, PZ), F32),
+            line,
+            line,
+        ),
+        [SMEM, VMEM, VMEM],
+    )(odd, table, field)
+    crossed = along(facing, "bx", both_ways([(i, i + 1) for i in range(1, count - 1, 2)]))
+    down = along(last_lane, "by", [(i, i + 1) for i in range(columns - 1)])
+    up = along(first_lane, "by", [(i + 1, i) for i in range(columns - 1)])
+    slot_rows = voxel_slot.reshape(groups, PZ)
+    sent = table
+    swapped = along(packed, "bx", swap)
+    ahead = along(sent, "bx", forward)
+    behind = along(sent, "bx", backward)
+
+    ints = functools.partial(jax.ShapeDtypeStruct, dtype=jnp.int32)
+    ordered, pos, info = kernel_call(
+        functools.partial(order_kernel, slots),
+        (
+            jax.ShapeDtypeStruct((slots, groups + WIDE // PZ + 1, 8, PZ), F32),
+            ints((groups, PZ)),
+            ints((2 * slots, groups)),
+        ),
+        [HBM] * 3,
+        [
+            pltpu.VMEM((groups, PZ), jnp.int32),
+            pltpu.VMEM((groups, PZ), jnp.int32),
+            pltpu.VMEM((3, groups, PZ), F32),
+            pltpu.VMEM((groups, PZ), jnp.int32),
+            pltpu.VMEM((groups * 8, PZ), F32),
+            pltpu.VMEM((groups, 8, PZ), jnp.int32),
+            pltpu.SMEM((2 * slots, groups), jnp.int32),
+            pltpu.SemaphoreType.DMA((4,)),
+        ],
+        cost=7.0,
+    )(*[
+        pltpu.with_memory_space_constraint(a, pltpu.HBM)
+        for a in (slot_rows, voxel_cell.reshape(groups, PZ), frac.reshape(3, groups, PZ))
+    ])
+    ahead, behind, swapped, ordered = lax.optimization_barrier((ahead, behind, swapped, ordered))
+
+    steps = [[m for m in (k, -k) if 2 * m > -lines] for k in range(1, lines // 2 + 1)]
+    places = [(0, 0), (0, 1)] + [(m, over) for step in steps for over in (0, 1) for m in step]
     my_slabs = lax.dynamic_index_in_dim(lists[:, 0, :], row, 0, keepdims=False)
-    far = jnp.array([k for _, k, _ in arrivals], jnp.int32)
-    over = jnp.array([k for _, _, k in arrivals], jnp.int32)
+    far = jnp.array([k for k, _ in places], jnp.int32)
+    over = jnp.array([k for _, k in places], jnp.int32)
     owners = ((row // 2 - far + count) % lines) * 2 + (row % 2 + over) % 2
     listed = owners[:, None] == my_slabs[None, :]
     plan = jnp.max(jnp.where(listed, jnp.arange(slots, dtype=jnp.int32)[None, :], -1), axis=1)
 
-    slot_rows = voxel_slot.reshape(groups, PZ)
-    ints = jax.ShapeDtypeStruct((groups, PZ), jnp.int32)
-    pos, dest, info = kernel_call(
-        functools.partial(rank_kernel, slots),
-        (ints, ints, jax.ShapeDtypeStruct((2 * slots, groups), jnp.int32)),
-        [VMEM],
-    )(slot_rows)
-    ordered = kernel_call(
-        functools.partial(sort_kernel, slots),
-        jax.ShapeDtypeStruct((slots, groups + WIDE // PZ, 8, PZ), F32),
-        [SMEM, VMEM, VMEM, VMEM],
-        [pltpu.VMEM((groups * 8, PZ), F32), pltpu.VMEM((groups, 8, PZ), jnp.int32)],
-    )(info, dest, voxel_cell.reshape(groups, PZ), frac.reshape(3, groups, PZ))
-    rotation = rotations(displace)
-
-    samples = None
-    cuts = [0] + [c for c in (2, 4, count - 1, count) if c <= count]
-    for first, last in zip(cuts[:-1], cuts[1:]):
-        blocks = [b for b, _, _ in arrivals[first:last]]
-        samples = sample(slots, first, blocks, plan, info, ordered, samples)
+    blocks = [table, swapped]
+    for k in range(1, lines // 2 + 1):
+        new = [ahead] + ([behind] if 2 * k < lines else [])
+        blocks += new + [along(block, "bx", swap) for block in new]
+        if 2 * (k + 1) <= lines:
+            ahead = along(ahead, "bx", forward)
+        if 2 * (k + 1) < lines:
+            behind = along(behind, "bx", backward)
+    samples = sample(slots, 0, blocks[:4], plan, info, ordered, None)
+    samples = sample(slots, 4, blocks[4:-1], plan, info, ordered, samples)
+    samples = sample(slots, count - 1, blocks[-1:], plan, info, ordered, samples)
+
+    rotation = kernel_call(
+        rotation_kernel,
+        jax.ShapeDtypeStruct((9, groups, PZ), F32),
+        [SMEM] + [VMEM] * 5,
+        [
+            pltpu.VMEM((3, groups + 16, PZ), F32),
+            pltpu.VMEM((3, groups, PZ), F32),
+            pltpu.VMEM((8, groups), F32),
+        ],
+    )(odd, field, swapped, crossed, down, up)
 
     result = kernel_call(
         functools.partial(finish_kernel, slots),
         jax.ShapeDtypeStruct((PARTS, groups, PZ), F32),
         [SMEM] + [VMEM] * 4,
-        [pltpu.VMEM((groups * 8, PZ), F32)],
+        [
+            pltpu.VMEM((groups * 8, PZ), F32),
+            pltpu.VMEM((PARTS, groups, PZ), F32),
+            pltpu.SemaphoreType.DMA((groups // SHARE,)),
+        ],
+        out_spec=HBM,
     )(info, slot_rows, pos, samples, rotation)
     return result.reshape(1, 1, PARTS, voxels)
 

time: 60.2 us -> 47.3 us (0.79)
  the two profiles are of different devices: /device:TPU:0 before, /device:TPU:1 now
where the time goes in v2:
time: 47.3 us; the launch traced here: 46.8 us
  Pallas kernels  22.1 us (47%)
  starting transfers between devices  17.9 us (38%)
  local copies, waits for them, and re-layouts  3.84 us (8%)
  waiting for transfers between devices  2.08 us (4%)
  other arithmetic  0.77 us (2%)
    ppermute x10, starting transfers between devices, along(): return lax.ppermute(values, axis, pairs)  17.9 us
    pallas_call x3, Pallas kernels, sample(): kernel_call(functools.partial(sample_kernel, slots, first, len(blocks), a...  11.7 us
    pallas_call x1, Pallas kernels, on_device(): kernel_call(functools.partial(order_kernel, slots), (jax.ShapeDtypeStruct...  5.79 us
    unnamed x16, local copies, waits for them, and re-layouts  3.65 us
    pallas_call x1, Pallas kernels, on_device(): kernel_call(functools.partial(finish_kernel, slots), jax.ShapeDtypeStruct...  2.38 us
    ppermute x10, waiting for transfers between devices, along(): return lax.ppermute(values, axis, pairs)  2.08 us
    pallas_call x1, Pallas kernels, on_device(): kernel_call(rotation_kernel, jax.ShapeDtypeStruct((9, groups, PZ), F32),...  1.52 us
  transfers between devices with their start and end apart: 10, of which 2 were waited for; matrix products, arithmetic and copies ran while one was open for 2% of the time, Pallas kernels for 39%

profile of v2, /device:TPU:1, one launch (start us, length us, event | category | flops | bytes accessed | tf_op | source)
XLA Modules:
  0.0 46.8 jit_solution(12810131911135917236)
XLA Ops:
  0.0 0.0 copy-start
  0.0 0.0 copy-start.1
  0.0 0.9 %copy-done.1 = f32[1,1,6,8192]{3,1,2,0:T(1,128)S(1)} copy-done((f32[1,1,6,8192]{3,1,2,0:T(1,128)S(1)}, f32[1,1,6,8192]{3,1,2,0:T(1,128)}, u32[]{:S(2)}) %copy-start.1) | copy-done | bytes 196632
  0.9 0.0 copy-start.3
  0.9 0.9 %copy-done.3 = f32[3,64,2,128]{3,2,1,0:T(2,128)S(1)} copy-done((f32[3,64,2,128]{3,2,1,0:T(2,128)S(1)}, f32[3,64,2,128]{3,2,1,0:T(2,128)}, u32[]{:S(2)}) %copy-start.3) | copy-done | bytes 196632
  1.9 0.7 %shard_map.83 = (f32[576,128]{1,0:T(8,128)S(1)}, f32[192,128]{1,0:T(8,128)}, f32[3,128]{1,0:T(4,128)S(1)}, f32[3,128]{1,0:T(4,128)S(1)}) custom-call(s32[1]{0:T(128)} %bitcast.4.odd_ref, f32[384,128]{1,0:T(8,128)S(1)} %bitcast.7, f32[3,128,128]{2,1,0:T(8,128)S(1)} %bitcast.11), custom_call_target="tpu_custom_call" | custom-call | bytes 3000000 | tf_op jit(solution)/shard_map/pallas_call | solution.py:396
  2.6 2.1 %collective-permute-start.2 = (f32[576,128]{1,0:T(8,128)S(1)}, f32[576,128]{1,0:T(8,128)S(1)}, u32[]{:S(2)}, u32[]{:S(2)}) collective-permute-start(f32[576,128]{1,0:T(8,128)S(1)} %get-tuple-element.18), channel_id=1, source_target_pairs={{0,4},{4,0},{8,12},{12,8},{16,20},{20,16},{24,28},{28,24},{1,5},{5... | collective-permute-start | bytes 884744 | tf_op jit(solution)/shard_map/ppermute | solution.py:343
  4.7 1.3 %collective-permute-start = (f32[384,128]{1,0:T(8,128)S(1)}, f32[384,128]{1,0:T(8,128)S(1)}, u32[]{:S(2)}, u32[]{:S(2)}) collective-permute-start(f32[384,128]{1,0:T(8,128)S(1)} %bitcast.8), channel_id=1, source_target_pairs={{0,8},{4,12},{8,16},{12,20},{16,24},{20,28},{24,0},{28,4},{1,9},{5... | collective-permute-start | bytes 589832 | tf_op jit(solution)/shard_map/ppermute | solution.py:343
  6.0 2.0 %collective-permute-start.1 = (f32[384,128]{1,0:T(8,128)S(1)}, f32[384,128]{1,0:T(8,128)S(1)}, u32[]{:S(2)}, u32[]{:S(2)}) collective-permute-start(f32[384,128]{1,0:T(8,128)S(1)} %bitcast.9), channel_id=1, source_target_pairs={{8,0},{12,4},{16,8},{20,12},{24,16},{28,20},{0,24},{4,28},{9,1},{1... | collective-permute-start | bytes 589832 | tf_op jit(solution)/shard_map/ppermute | solution.py:343
  8.0 5.8 %shard_map.82 = (f32[4,137,8,128]{3,2,1,0:T(8,128)S(1)}, s32[128,128]{1,0:T(8,128)S(1)}, s32[8,128]{1,0:T(8,128)S(1)}) custom-call(s32[128,128]{1,0:T(8,128)} %bitcast.13, s32[128,128]{1,0:T(8,128)} %bitcast.16, f32[3,128,128]{2,1,0:T(8,128)} %bitcast.15), custom_call_target="tpu_custom_call" | custom-call | bytes 21000000 | tf_op jit(solution)/shard_map/pallas_call | solution.py:416
  13.8 0.0 copy-start.6
  13.8 0.6 %copy-done.6 = s32[128,128]{1,0:T(8,128)} copy-done((s32[128,128]{1,0:T(8,128)}, s32[128,128]{1,0:T(8,128)S(1)}, u32[]{:S(2)}) %copy-start.6) | copy-done | bytes 65560
  14.4 0.0 collective-permute-done.refs_2_
  14.4 1.9 %collective-permute-done.1.refs_3_ = f32[384,128]{1,0:T(8,128)S(1)} collective-permute-done((f32[384,128]{1,0:T(8,128)S(1)}, f32[384,128]{1,0:T(8,128)S(1)}, u32[]{:S(2)}, u32[]{:S(2)}) %collective-permute-start.1) | collective-permute-done | bytes 196640 | tf_op jit(solution)/shard_map/ppermute | solution.py:343
  16.4 0.0 collective-permute-done.2.refs_1_.swapped_ref
  16.4 1.5 %collective-permute-start.3 = (f32[384,128]{1,0:T(8,128)S(1)}, f32[384,128]{1,0:T(8,128)S(1)}, u32[]{:S(2)}, u32[]{:S(2)}) collective-permute-start(f32[384,128]{1,0:T(8,128)S(1)} %collective-permute-done.refs_2_), channel_id=1, source_target_pairs={{0,8},{4,12},{8,16},{12,20},{16,24},{20,28},{24,0},{28,4},{1,9},{5... | collective-permute-start | bytes 589832 | tf_op jit(solution)/shard_map/ppermute | solution.py:343
  17.8 1.3 %collective-permute-start.7 = (f32[192,128]{1,0:T(8,128)}, f32[192,128]{1,0:T(8,128)}, u32[]{:S(2)}, u32[]{:S(2)}) collective-permute-start(f32[192,128]{1,0:T(8,128)} %get-tuple-element.24), channel_id=1, source_target_pairs={{4,8},{12,16},{20,24},{8,4},{16,12},{24,20},{5,9},{13,17},{21,25},... | collective-permute-start | bytes 294920 | tf_op jit(solution)/shard_map/ppermute | solution.py:343
  19.1 3.8 %collective-permute-start.8 = (f32[3,128]{1,0:T(4,128)S(1)}, f32[3,128]{1,0:T(4,128)S(1)}, u32[]{:S(2)}, u32[]{:S(2)}) collective-permute-start(f32[3,128]{1,0:T(4,128)S(1)} %get-tuple-element.25), channel_id=1, source_target_pairs={{0,1},{1,2},{2,3},{4,5},{5,6},{6,7},{8,9},{9,10},{10,11},{12,13},{... | collective-permute-start | bytes 4616 | tf_op jit(solution)/shard_map/ppermute | solution.py:343
  22.9 2.6 %collective-permute-start.5 = (f32[384,128]{1,0:T(8,128)S(1)}, f32[384,128]{1,0:T(8,128)S(1)}, u32[]{:S(2)}, u32[]{:S(2)}) collective-permute-start(f32[384,128]{1,0:T(8,128)S(1)} %collective-permute-done.refs_2_), channel_id=1, source_target_pairs={{0,4},{4,0},{8,12},{12,8},{16,20},{20,16},{24,28},{28,24},{1,5},{5... | collective-permute-start | bytes 589832 | tf_op jit(solution)/shard_map/ppermute | solution.py:343
  25.5 0.1 collective-permute-start.6
  25.6 0.0 collective-permute-done.3.refs_2_
  25.6 1.4 %collective-permute-start.4 = (f32[384,128]{1,0:T(8,128)S(1)}, f32[384,128]{1,0:T(8,128)S(1)}, u32[]{:S(2)}, u32[]{:S(2)}) collective-permute-start(f32[384,128]{1,0:T(8,128)S(1)} %collective-permute-done.3.refs_2_), channel_id=1, source_target_pairs={{0,4},{4,0},{8,12},{12,8},{16,20},{20,16},{24,28},{28,24},{1,5},{5... | collective-permute-start | bytes 589832 | tf_op jit(solution)/shard_map/ppermute | solution.py:343
  27.0 0.7 %fusion = s32[8]{0:T(128)S(1)} fusion(s32[8]{0:T(128)} %constant.67.clone, s32[8]{0:T(128)} %constant.74, s32[]{:T(128)} %select_n.33, s32[]{:T(128)S(6)} %select_n.31), kind=kLoop, calls=%fused_computation.8 | loop fusion | flops 216 | bytes 104 | tf_op jit(solution)/shard_map/add | solution.py:446
  27.7 0.0 copy-done
  27.7 0.2 dynamic-slice_reduce_fusion
  27.9 0.0 collective-permute-done.8.down_ref
  27.9 1.9 %collective-permute-start.9 = (f32[3,128]{1,0:T(4,128)S(1)}, f32[3,128]{1,0:T(4,128)S(1)}, u32[]{:S(2)}, u32[]{:S(2)}) collective-permute-start(f32[3,128]{1,0:T(4,128)S(1)} %get-tuple-element.26), channel_id=1, source_target_pairs={{1,0},{2,1},{3,2},{5,4},{6,5},{7,6},{9,8},{10,9},{11,10},{13,12},{... | collective-permute-start | bytes 4616 | tf_op jit(solution)/shard_map/ppermute | solution.py:343
  29.8 0.1 select_reduce_fusion.plan_ref
  29.9 0.0 copy-start.2
  29.9 0.9 %copy-done.2 = f32[1,1,6,8192]{3,1,2,0:T(1,128)S(1)} copy-done((f32[1,1,6,8192]{3,1,2,0:T(1,128)S(1)}, f32[1,1,6,8192]{3,1,2,0:T(1,128)}, u32[]{:S(2)}) %copy-start.2) | copy-done | bytes 196632
  30.8 0.0 copy-start.4
  30.8 2.7 %shard_map.84.refs_3_ = f32[4,137,8,128]{3,2,1,0:T(8,128)S(1)} custom-call(s32[8]{0:T(128)S(1)} %select_reduce_fusion.plan_ref, s32[8,128]{1,0:T(8,128)S(1)} %get-tuple-element.16.info_ref, f32[4,137,8,128]{3,2,1,0:T(8,128)S(1)} %get-tuple-element.20.sorted_ref, f32[384,128]{1,0:T(8,128)S(1)} %bitcast.10, ...), custom_call_target="tpu_custom_call" | custom-call | bytes 30000000 | tf_op jit(solution)/shard_map/pallas_call | solution.py:221
  33.6 0.0 collective-permute-done.9.up_ref
  33.6 0.0 collective-permute-done.7.crossed_ref
  33.6 0.0 copy-done.4
  33.6 1.5 %shard_map.87.rotation_ref = f32[9,128,128]{2,1,0:T(8,128)S(1)} custom-call(s32[1]{0:T(128)} %bitcast.4.odd_ref, f32[3,128,128]{2,1,0:T(8,128)S(1)} %bitcast.12, f32[576,128]{1,0:T(8,128)S(1)} %collective-permute-done.2.refs_1_.swapped_ref, f32[192,128]{1,0:T(8,128)} %collective-permute-done.7.crossed_ref, f32[3,128]{1,0:T(4,128)S(1)} %collective-permute-done.8.down_ref, ...), custom_call_target="tpu_custom_call" | custom-call | bytes 3000000 | tf_op jit(solution)/shard_map/pallas_call | solution.py:462
  35.1 0.0 collective-permute-done.5.refs_0_
  35.1 0.1 collective-permute-done.6.refs_1_
  35.3 8.3 %shard_map.85.refs_1_ = f32[4,137,8,128]{3,2,1,0:T(8,128)S(1)} custom-call(s32[8]{0:T(128)S(1)} %select_reduce_fusion.plan_ref, s32[8,128]{1,0:T(8,128)S(1)} %get-tuple-element.16.info_ref, f32[4,137,8,128]{3,2,1,0:T(8,128)S(1)} %get-tuple-element.20.sorted_ref, f32[384,128]{1,0:T(8,128)S(1)} %collective-permute-done.5.refs_0_, ...), custom_call_target="tpu_custom_call", output_to_operand_aliasing={{}: (6, {})} | custom-call | bytes 22500000 | tf_op jit(solution)/shard_map/pallas_call | solution.py:221
  43.6 0.0 copy-start.5
  43.6 0.0 copy-start.7
  43.6 0.0 collective-permute-done.4.refs_0_
  43.6 0.6 %shard_map.86.samples_ref = f32[4,137,8,128]{3,2,1,0:T(8,128)S(1)} custom-call(s32[8]{0:T(128)S(1)} %select_reduce_fusion.plan_ref, s32[8,128]{1,0:T(8,128)S(1)} %get-tuple-element.16.info_ref, f32[4,137,8,128]{3,2,1,0:T(8,128)S(1)} %get-tuple-element.20.sorted_ref, f32[384,128]{1,0:T(8,128)S(1)} %collective-permute-done.4.refs_0_, ...), custom_call_target="tpu_custom_call", output_to_operand_aliasing={{}: (4, {})} | custom-call | bytes 7500000 | tf_op jit(solution)/shard_map/pallas_call | solution.py:221
  44.2 0.2 copy-done.5
  44.4 0.0 copy-done.7
  44.5 2.4 %shard_map.88 = f32[6,128,128]{2,1,0:T(8,128)} custom-call(s32[8,128]{1,0:T(8,128)S(1)} %get-tuple-element.16.info_ref, s32[128,128]{1,0:T(8,128)S(1)} %bitcast.14, s32[128,128]{1,0:T(8,128)S(1)} %copy-done.7, f32[4,137,8,128]{3,2,1,0:T(8,128)S(1)} %shard_map.86.samples_ref, f32[9,128,128]{2,1,0:T(8,128)S(1)} %shard_map.87.rotation_ref), custom_call_target="tpu_custom_call" | custom-call | bytes 3000000 | tf_op jit(solution)/shard_map/pallas_call | solution.py:473
Async XLA Ops:
  0.0 27.7 %copy-start = (s32[8,1,4]{0,2,1:T(4,128)S(1)}, s32[8,1,4]{0,2,1:T(4,128)}, u32[]{:S(2)}) copy-start(s32[8,1,4]{0,2,1:T(4,128)} %param.9) | copy-start | bytes 388
  0.0 0.9 %copy-start.1 = (f32[1,1,6,8192]{3,1,2,0:T(1,128)S(1)}, f32[1,1,6,8192]{3,1,2,0:T(1,128)}, u32[]{:S(2)}) copy-start(f32[1,1,6,8192]{3,1,2,0:T(1,128)} %param.8) | copy-start | bytes 589828
  0.9 0.9 %copy-start.3 = (f32[3,64,2,128]{3,2,1,0:T(2,128)S(1)}, f32[3,64,2,128]{3,2,1,0:T(2,128)}, u32[]{:S(2)}) copy-start(f32[3,64,2,128]{3,2,1,0:T(2,128)} %param.13) | copy-start | bytes 589828
  2.6 13.8 %collective-permute-start.2 = (f32[576,128]{1,0:T(8,128)S(1)}, f32[576,128]{1,0:T(8,128)S(1)}, u32[]{:S(2)}, u32[]{:S(2)}) collective-permute-start(f32[576,128]{1,0:T(8,128)S(1)} %get-tuple-element.18), channel_id=1, source_target_pairs={{0,4},{4,0},{8,12},{12,8},{16,20},{20,16},{24,28},{28,24},{1,5},{5... | collective-permute-start | bytes 884744 | tf_op jit(solution)/shard_map/ppermute | solution.py:343
  4.7 9.8 %collective-permute-start = (f32[384,128]{1,0:T(8,128)S(1)}, f32[384,128]{1,0:T(8,128)S(1)}, u32[]{:S(2)}, u32[]{:S(2)}) collective-permute-start(f32[384,128]{1,0:T(8,128)S(1)} %bitcast.8), channel_id=1, source_target_pairs={{0,8},{4,12},{8,16},{12,20},{16,24},{20,28},{24,0},{28,4},{1,9},{5... | collective-permute-start | bytes 589832 | tf_op jit(solution)/shard_map/ppermute | solution.py:343
  6.0 10.4 %collective-permute-start.1 = (f32[384,128]{1,0:T(8,128)S(1)}, f32[384,128]{1,0:T(8,128)S(1)}, u32[]{:S(2)}, u32[]{:S(2)}) collective-permute-start(f32[384,128]{1,0:T(8,128)S(1)} %bitcast.9), channel_id=1, source_target_pairs={{8,0},{12,4},{16,8},{20,12},{24,16},{28,20},{0,24},{4,28},{9,1},{1... | collective-permute-start | bytes 589832 | tf_op jit(solution)/shard_map/ppermute | solution.py:343
  13.8 0.6 %copy-start.6 = (s32[128,128]{1,0:T(8,128)}, s32[128,128]{1,0:T(8,128)S(1)}, u32[]{:S(2)}) copy-start(s32[128,128]{1,0:T(8,128)S(1)} %get-tuple-element.17.pos_ref) | copy-start | bytes 196612
  16.4 9.3 %collective-permute-start.3 = (f32[384,128]{1,0:T(8,128)S(1)}, f32[384,128]{1,0:T(8,128)S(1)}, u32[]{:S(2)}, u32[]{:S(2)}) collective-permute-start(f32[384,128]{1,0:T(8,128)S(1)} %collective-permute-done.refs_2_), channel_id=1, source_target_pairs={{0,8},{4,12},{8,16},{12,20},{16,24},{20,28},{24,0},{28,4},{1,9},{5... | collective-permute-start | bytes 589832 | tf_op jit(solution)/shard_map/ppermute | solution.py:343
  17.8 15.7 %collective-permute-start.7 = (f32[192,128]{1,0:T(8,128)}, f32[192,128]{1,0:T(8,128)}, u32[]{:S(2)}, u32[]{:S(2)}) collective-permute-start(f32[192,128]{1,0:T(8,128)} %get-tuple-element.24), channel_id=1, source_target_pairs={{4,8},{12,16},{20,24},{8,4},{16,12},{24,20},{5,9},{13,17},{21,25},... | collective-permute-start | bytes 294920 | tf_op jit(solution)/shard_map/ppermute | solution.py:343
  19.1 8.8 %collective-permute-start.8 = (f32[3,128]{1,0:T(4,128)S(1)}, f32[3,128]{1,0:T(4,128)S(1)}, u32[]{:S(2)}, u32[]{:S(2)}) collective-permute-start(f32[3,128]{1,0:T(4,128)S(1)} %get-tuple-element.25), channel_id=1, source_target_pairs={{0,1},{1,2},{2,3},{4,5},{5,6},{6,7},{8,9},{9,10},{10,11},{12,13},{... | collective-permute-start | bytes 4616 | tf_op jit(solution)/shard_map/ppermute | solution.py:343
  22.9 12.2 %collective-permute-start.5 = (f32[384,128]{1,0:T(8,128)S(1)}, f32[384,128]{1,0:T(8,128)S(1)}, u32[]{:S(2)}, u32[]{:S(2)}) collective-permute-start(f32[384,128]{1,0:T(8,128)S(1)} %collective-permute-done.refs_2_), channel_id=1, source_target_pairs={{0,4},{4,0},{8,12},{12,8},{16,20},{20,16},{24,28},{28,24},{1,5},{5... | collective-permute-start | bytes 589832 | tf_op jit(solution)/shard_map/ppermute | solution.py:343
  25.5 9.7 %collective-permute-start.6 = (f32[384,128]{1,0:T(8,128)S(1)}, f32[384,128]{1,0:T(8,128)}, u32[]{:S(2)}, u32[]{:S(2)}) collective-permute-start(f32[384,128]{1,0:T(8,128)S(1)} %collective-permute-done.1.refs_3_), channel_id=1, source_target_pairs={{0,4},{4,0},{8,12},{12,8},{16,20},{20,16},{24,28},{28,24},{1,5},{5... | collective-permute-start | bytes 589832 | tf_op jit(solution)/shard_map/ppermute | solution.py:343
  25.6 18.0 %collective-permute-start.4 = (f32[384,128]{1,0:T(8,128)S(1)}, f32[384,128]{1,0:T(8,128)S(1)}, u32[]{:S(2)}, u32[]{:S(2)}) collective-permute-start(f32[384,128]{1,0:T(8,128)S(1)} %collective-permute-done.3.refs_2_), channel_id=1, source_target_pairs={{0,4},{4,0},{8,12},{12,8},{16,20},{20,16},{24,28},{28,24},{1,5},{5... | collective-permute-start | bytes 589832 | tf_op jit(solution)/shard_map/ppermute | solution.py:343
  27.9 5.7 %collective-permute-start.9 = (f32[3,128]{1,0:T(4,128)S(1)}, f32[3,128]{1,0:T(4,128)S(1)}, u32[]{:S(2)}, u32[]{:S(2)}) collective-permute-start(f32[3,128]{1,0:T(4,128)S(1)} %get-tuple-element.26), channel_id=1, source_target_pairs={{1,0},{2,1},{3,2},{5,4},{6,5},{7,6},{9,8},{10,9},{11,10},{13,12},{... | collective-permute-start | bytes 4616 | tf_op jit(solution)/shard_map/ppermute | solution.py:343
  29.9 0.9 %copy-start.2 = (f32[1,1,6,8192]{3,1,2,0:T(1,128)S(1)}, f32[1,1,6,8192]{3,1,2,0:T(1,128)}, u32[]{:S(2)}) copy-start(f32[1,1,6,8192]{3,1,2,0:T(1,128)} %param.8) | copy-start | bytes 589828
  30.8 2.8 %copy-start.4 = (f32[3,64,2,128]{3,2,1,0:T(2,128)S(1)}, f32[3,64,2,128]{3,2,1,0:T(2,128)}, u32[]{:S(2)}) copy-start(f32[3,64,2,128]{3,2,1,0:T(2,128)} %param.13) | copy-start | bytes 589828
  43.6 0.8 %copy-start.5 = (s32[1,1,16384]{2,1,0:T(1,128)S(1)}, s32[1,1,16384]{2,1,0:T(1,128)}, u32[]{:S(2)}) copy-start(s32[1,1,16384]{2,1,0:T(1,128)} %param.10) | copy-start | bytes 196612
  43.6 0.9 %copy-start.7 = (s32[128,128]{1,0:T(8,128)S(1)}, s32[128,128]{1,0:T(8,128)}, u32[]{:S(2)}) copy-start(s32[128,128]{1,0:T(8,128)} %copy-done.6) | copy-start | bytes 196612
